TPU v7x, 256 devices: a whole 4x4x8 slice. The times are simulated.
256 devices in a mesh: wave: 64 (over z, y, core), lev: 4 (over x).
Axes of the slice: x: 4, y: 4, z: 8, core: 2. Of those that a mesh axis runs over, the one named last changes fastest.
Arguments:
- fourier: float32 [128, 4, 72, 2560], P(None, None, 'lev', 'wave'), may hold values from -6 to 6
- legendre: float32 [128, 1280, 2560], P('wave', None, 'lev'), may hold values from -0.125 to 0.125
- weights: float32 [2560], replicated, may hold values from 0.25 to 2
- points: int32 [2560], replicated, may hold values from 16 to 3199
- zonal: int32 [128], replicated, may hold values from 0 to 1279, as said below
- pressure_balance_matrix: float32 [72, 72], replicated, may hold values from -0.75 to 0.75
- modes: float32 [72, 72], replicated, may hold values from -0.75 to 0.75
- project: float32 [72, 72], replicated, may hold values from -0.75 to 0.75
- eigen: float32 [72], replicated, may hold values from 0.1 to 10
- thermal_reply_matrix: float32 [72, 72], replicated, may hold values from -0.75 to 0.75
Outputs:
- spectral: float32 [128, 4, 72, 1280], P('wave', None, 'lev')
- fourier_new: float32 [128, 4, 72, 2560], P(None, None, 'lev', 'wave')
Inputs may be any that keep to these rules, and one draw needn't show every extreme that they name: Distinct zonal wavenumbers; slot s belongs to wave index s // 2; 0 and 1279 each appear in one slot.
All inputs are finite; a program needn't handle non-finite values.
Results may differ from a plain program's by a relative error of at most 0.000088.
Values sent between devices are 32-bit elements; how exact they have to be, the bound alone decides.
A program may use at most 128 MiB of HBM per device.

v0:
```python
import jax
import jax.numpy as jnp
from jax import lax
from jax.sharding import PartitionSpec as P


def helmholtz(
    harmonic_amplitudes, pressure_balance_matrix, modes, project, eigen, thermal_reply_matrix, total
):
    highest = lax.Precision.HIGHEST
    wavenumber = jnp.arange(total, dtype=jnp.int32)
    timestep_weighting = (wavenumber * (wavenumber + 1)).astype(jnp.float32) * (
        4.0 / (total * (total + 1))
    )
    velocity_spreading = harmonic_amplitudes[:, 0:2]
    thermal_state = harmonic_amplitudes[:, 2:4]
    tendency_sources = velocity_spreading + timestep_weighting * jnp.einsum(
        "kl,mcln->mckn", pressure_balance_matrix, thermal_state, precision=highest
    )
    modal = jnp.einsum("kl,mcln->mckn", project, tendency_sources, precision=highest) / (
        1.0 + eigen[:, None] * timestep_weighting
    )
    revised_spreading = jnp.einsum("kl,mcln->mckn", modes, modal, precision=highest)
    revised_thermal = thermal_state - jnp.einsum(
        "kl,mcln->mckn", thermal_reply_matrix, revised_spreading, precision=highest
    )
    return jnp.concatenate([revised_spreading, revised_thermal], axis=1)


def on_device(
    fourier,
    legendre,
    weights,
    points,
    zonal,
    pressure_balance_matrix,
    modes,
    project,
    eigen,
    thermal_reply_matrix,
):
    highest = lax.Precision.HIGHEST
    wave_count = legendre.shape[0]
    total = legendre.shape[1]
    lat_local = fourier.shape[3]
    lev_count = fourier.shape[2]
    wave_index = lax.axis_index("wave")
    lev_index = lax.axis_index("lev")
    band_start = wave_index * lat_local
    band_points = lax.dynamic_slice_in_dim(points, band_start, lat_local)
    band_weights = lax.dynamic_slice_in_dim(weights, band_start, lat_local)
    present = (2 * zonal[:, None] < band_points[None, :])[:, None, None, :]
    scaled = jnp.where(present, fourier, 0.0) * band_weights
    my_zonal = lax.dynamic_slice_in_dim(zonal, wave_index * wave_count, wave_count)
    wavenumber = jnp.arange(total, dtype=jnp.int32)
    living = (wavenumber[None, :] >= my_zonal[:, None])[:, None, None, :]
    columns = lax.all_to_all(scaled, "wave", split_axis=0, concat_axis=3, tiled=True)
    blocks = lax.all_to_all(columns, "lev", split_axis=3, concat_axis=2, tiled=True)
    harmonic_amplitudes = jnp.einsum("mclj,mnj->mcln", blocks, legendre, precision=highest)
    harmonic_amplitudes = jnp.where(living, harmonic_amplitudes, 0.0)
    summed = lax.psum(harmonic_amplitudes, "lev")
    corrected = helmholtz(
        summed, pressure_balance_matrix, modes, project, eigen, thermal_reply_matrix, total
    )
    own_levels = lax.dynamic_slice_in_dim(corrected, lev_index * lev_count, lev_count, 2)
    quarter = jnp.einsum("mcln,mnj->mclj", corrected, legendre, precision=highest)
    synthesis = lax.all_to_all(quarter, "lev", split_axis=2, concat_axis=3, tiled=True)
    banded = lax.all_to_all(synthesis, "wave", split_axis=3, concat_axis=0, tiled=True)
    fourier_new = jnp.where(present, banded, 0.0)
    return (own_levels, fourier_new)


def solution(mesh):
    return jax.shard_map(
        on_device,
        mesh=mesh,
        in_specs=(
            P(None, None, "lev", "wave"),
            P("wave", None, "lev"),
            P(),
            P(),
            P(),
            P(),
            P(),
            P(),
            P(),
            P(),
        ),
        out_specs=(P("wave", None, "lev", None), P(None, None, "lev", "wave")),
        check_vma=False,
    )
```

profile of v0, /device:TPU:1, one launch (start us, length us, event | category | flops | bytes accessed | tf_op | source)
XLA Modules:
  0.0 424.9 jit_solution(12392496019470711707)
XLA Ops:
  7.2 0.0 copy-start
  7.2 0.8 dynamic_slice.14
  8.0 0.8 dynamic_slice.13
  8.7 0.7 broadcast_multiply_fusion
  9.4 0.1 broadcast_compare_fusion
  9.5 1.6 select_multiply_fusion
  11.0 3.6 copy.54
  14.6 8.7 %reshape.94 = f32[64,1,5760]{2,1,0:T(1,128)S(1)} reshape(f32[128,18,4,40]{3,2,1,0:T(4,128)} %bitcast.75) | data formatting | bytes 2949120
  23.3 50.2 %all_to_all.72 = f32[64,1,5760]{2,1,0:T(1,128)S(1)} all-to-all(f32[64,1,5760]{2,1,0:T(1,128)S(1)} %reshape.94), channel_id=1, replica_groups=mesh['wave'=64,'lev'=4] {'wave'}, dimensions={0} | all-to-all | bytes 2949120 | tf_op jit(solution)/shard_map/all_to_all | solution.py:57
  73.5 0.5 broadcast.64
  74.0 4.2 reduce
  78.2 8.2 %reshape.95 = f32[128,18,4,40]{3,2,1,0:T(4,128)} reshape(f32[64,5760]{1,0:T(8,128)S(1)} %reduce) | data formatting | bytes 2949120
  86.4 5.5 %copy.55 = f32[128,4,18,40]{3,0,2,1:T(8,128)} copy(f32[128,4,18,40]{3,1,2,0:T(4,128)} %bitcast.76) | data formatting | bytes 2949120 | tf_op jit(solution)/shard_map/all_to_all | solution.py:57
  91.9 12.0 %copy.74 = f32[2,4,18,64,40]{2,1,0,4,3:T(4,128)} copy(f32[2,4,18,64,40]{4,0,3,2,1:T(2,128)} %bitcast.78) | data formatting | bytes 2949120 | tf_op jit(solution)/shard_map/all_to_all | solution.py:57
  103.9 15.9 %reshape.96 = f32[4,1,92160]{2,1,0:T(1,128)} reshape(f32[2560,2,4,18]{3,2,1,0:T(4,128)} %bitcast.69) | data formatting | bytes 2949120
  119.8 4.1 all-to-all-start.1
  123.9 0.5 all-reduce.2.cloned.1.call-start
  124.4 0.1 dynamic_slice.12
  124.5 0.1 iota_compare_fusion
  124.6 17.4 %all-to-all-done.1 = f32[4,1,92160]{2,1,0:T(1,128)S(1)} async-done(((f32[4,1,92160]{2,1,0:T(1,128)}), f32[4,1,92160]{2,1,0:T(1,128)S(1)}, u32[]{:S(2)}, u32[]{:S(2)}) %all-to-all-start.1) | async-done | bytes 1474592 | tf_op jit(solution)/shard_map/all_to_all | solution.py:58
  141.9 4.9 %reduce.1 = f32[4,92160]{1,0:T(4,128)S(1)} reduce(f32[4,1,92160]{2,1,0:T(1,128)S(1)} %all-to-all-done.1, f32[]{:T(128)} %broadcast.64), dimensions={1}, to_apply=%all_to_all.56.reduce_sub_computation | reduce | bytes 2949124 | tf_op jit(solution)/shard_map/all_to_all | solution.py:58
  146.9 18.7 %reshape.97 = f32[2560,2,4,18]{3,2,1,0:T(4,128)} reshape(f32[4,92160]{1,0:T(4,128)S(1)} %reduce.1) | data formatting | bytes 2949120
  165.6 7.6 %copy.59 = f32[2,4,4,18,640]{4,1,3,2,0:T(4,128)S(1)} copy(f32[2,4,4,18,640]{3,1,0,4,2:T(4,128)} %bitcast.70) | data formatting | bytes 2949120 | tf_op jit(solution)/shard_map/all_to_all | solution.py:58
  173.2 10.6 %fusion.4 = f32[2,4,72,1280]{3,2,1,0:T(8,128)} fusion(f32[2,1280,640]{2,1,0:T(8,128)} %param.11, f32[2,4,72,640]{3,1,2,0:T(4,128)S(1)} %bitcast.80, pred[2,1280]{1,0:T(4,128)(4,1)S(1)} %iota_compare_fusion), kind=kOutput, calls=%fused_computation.4 | convolution fusion | flops 5663047680 | bytes 10979840 | tf_op jit(solution)/shard_map/mclj,mnj->mcln/dot_general | solution.py:59
  183.9 0.0 all-reduce.2.cloned.1.call-update
  183.9 0.6 copy-done.5
  184.5 0.1 multiply_add_fusion
  184.6 74.0 %all-reduce.2.cloned.1.call-done = f32[2,4,72,1280]{3,2,1,0:T(8,128)} async-done(((f32[2,4,72,1280]{3,2,1,0:T(8,128)}), f32[2,4,72,1280]{3,2,1,0:T(8,128)}) %all-reduce.2.cloned.1.call-update) | async-done | bytes 2949136 | tf_op jit(solution)/shard_map/psum | solution.py:61
  258.6 3.5 fusion.8
  262.1 1.5 fusion.10
  263.7 1.5 convolution_bitcast_fusion.1
  265.1 0.3 copy-done.2
  265.5 1.5 fusion.9
  267.0 7.7 %fusion = f32[2,4,72,640]{3,2,1,0:T(8,128)S(1)} fusion(f32[2,1280,640]{2,1,0:T(8,128)S(1)} %bitcast.74, f32[2,2,72,1280]{3,2,1,0:T(8,128)S(1)} %fusion.9, f32[2,2,72,1280]{3,2,1,0:T(8,128)S(1)} %convolution_bitcast_fusion.1), kind=kOutput, calls=%fused_computation | convolution fusion | flops 5663047680 | bytes 10977280 | tf_op jit(solution)/shard_map/mcln,mnj->mclj/dot_general | solution.py:66
  274.7 0.4 copy.61
  275.1 22.3 %all_to_all.73 = f32[2,4,72,640]{3,1,0,2:T(4,128)} all-to-all(f32[2,4,72,640]{3,1,0,2:T(4,128)S(1)} %copy.61), channel_id=1, replica_groups=mesh['wave'=64,'lev'=4] {'lev'}, dimensions={2} | all-to-all | bytes 2949120 | tf_op jit(solution)/shard_map/all_to_all | solution.py:67
  297.4 8.3 %copy.78 = f32[2,4,18,4,640]{2,1,0,4,3:T(4,128)} copy(f32[2,4,18,4,640]{4,1,0,2,3:T(4,128)} %bitcast.81) | data formatting | bytes 2949120 | tf_op jit(solution)/shard_map/all_to_all | solution.py:67
  305.7 14.2 %reshape.98 = f32[64,1,5760]{2,1,0:T(1,128)} reshape(f32[2560,2,4,18]{3,2,1,0:T(4,128)} %bitcast.71) | data formatting | bytes 2949120
  320.0 12.2 %all-to-all-start.3 = ((f32[64,1,5760]{2,1,0:T(1,128)}), f32[64,1,5760]{2,1,0:T(1,128)}, u32[]{:S(2)}, u32[]{:S(2)}) async-start(f32[64,1,5760]{2,1,0:T(1,128)} %reshape.98), calls=%async_computation.3 | async-start | bytes 2949120 | tf_op jit(solution)/shard_map/all_to_all | solution.py:68
  332.1 0.1 fusion.12
  332.2 1.1 copy.68
  333.4 35.5 %all-to-all-done.3 = f32[64,1,5760]{2,1,0:T(1,128)} async-done(((f32[64,1,5760]{2,1,0:T(1,128)}), f32[64,1,5760]{2,1,0:T(1,128)}, u32[]{:S(2)}, u32[]{:S(2)}) %all-to-all-start.3) | async-done | bytes 1474592 | tf_op jit(solution)/shard_map/all_to_all | solution.py:68
  368.9 5.5 %reduce.2 = f32[64,5760]{1,0:T(8,128)S(1)} reduce(f32[64,1,5760]{2,1,0:T(1,128)} %all-to-all-done.3, f32[]{:T(128)} %broadcast.64), dimensions={1}, to_apply=%all_to_all.64.reduce_sub_computation | reduce | bytes 2949124 | tf_op jit(solution)/shard_map/all_to_all | solution.py:68
  374.4 16.2 %reshape.99 = f32[2560,2,4,18]{3,2,1,0:T(4,128)} reshape(f32[64,5760]{1,0:T(8,128)S(1)} %reduce.2) | data formatting | bytes 2949120
  390.6 13.8 %copy.79 = f32[2,4,18,64,40]{4,3,1,2,0:T(8,128)} copy(f32[2,4,18,64,40]{2,1,0,4,3:T(4,128)} %bitcast.72) | data formatting | bytes 2949120 | tf_op jit(solution)/shard_map/all_to_all | solution.py:68
  404.4 8.9 %copy.66 = f32[64,2,4,18,40]{4,1,0,3,2:T(2,128)} copy(f32[64,2,4,18,40]{4,0,2,3,1:T(8,128)} %bitcast.79) | data formatting | bytes 2949120 | tf_op jit(solution)/shard_map/all_to_all | solution.py:68
  413.3 3.0 copy.67
  416.4 1.2 broadcast_select_fusion
  (19 shorter events, 0.1 us)
Async XLA Ops:
  7.2 251.4 %copy-start = (f32[72,72]{1,0:T(8,128)S(1)}, f32[72,72]{1,0:T(8,128)}, u32[]{:S(2)}) copy-start(f32[72,72]{1,0:T(8,128)} %param.15) | copy-start | bytes 62212
  119.8 4.6 %copy-start.7 = (s32[128]{0:T(128)S(1)}, s32[128]{0:T(128)}, u32[]{:S(2)}) copy-start(s32[128]{0:T(128)} %param.14) | copy-start | bytes 1540
  119.8 22.1 %all-to-all-start.1 = ((f32[4,1,92160]{2,1,0:T(1,128)}), f32[4,1,92160]{2,1,0:T(1,128)S(1)}, u32[]{:S(2)}, u32[]{:S(2)}) async-start(f32[4,1,92160]{2,1,0:T(1,128)} %reshape.96), calls=%async_computation.1 | async-start | bytes 2949120 | tf_op jit(solution)/shard_map/all_to_all | solution.py:58
  123.9 134.7 %all-reduce.2.cloned.1.call-start = ((), (), s32[]{:S(2)}) async-start(), calls=%async_computation.4 | async-start | bytes 5898240 | tf_op jit(solution)/shard_map/psum | solution.py:61
  183.9 0.7 copy-start.5
  184.6 77.5 %copy-start.6 = (f32[72,72]{1,0:T(8,128)S(1)}, f32[72,72]{1,0:T(8,128)}, u32[]{:S(2)}) copy-start(f32[72,72]{1,0:T(8,128)} %param.17) | copy-start | bytes 62212
  258.6 8.4 %slice-start = ((s8[6553600]{0:T(1024)(128)(4,1)}), s8[4194304]{0:T(1024)(128)(4,1)S(1)}, s32[]{:S(2)}) async-start(s8[6553600]{0:T(1024)(128)(4,1)} %bitcast.73), calls=%async_computation.5 | async-start | bytes 8388608
  262.1 1.5 copy-start.4
  262.1 4.8 %slice-start.1 = ((s8[6553600]{0:T(1024)(128)(4,1)}), s8[2359296]{0:T(1024)(128)(4,1)S(1)}, s32[]{:S(2)}) async-start(s8[6553600]{0:T(1024)(128)(4,1)} %bitcast.73), calls=%async_computation.6 | async-start | bytes 4718592
  263.6 1.8 copy-start.2
  263.7 1.8 copy-start.3
  320.0 49.0 %all-to-all-start.3 = ((f32[64,1,5760]{2,1,0:T(1,128)}), f32[64,1,5760]{2,1,0:T(1,128)}, u32[]{:S(2)}, u32[]{:S(2)}) async-start(f32[64,1,5760]{2,1,0:T(1,128)} %reshape.98), calls=%async_computation.3 | async-start | bytes 2949120 | tf_op jit(solution)/shard_map/all_to_all | solution.py:68
  413.3 4.2 copy-start.1
Sparse Core Ops, SparseCore 0:
  184.0 74.5 all-reduce.1
where the time goes:
time: 430 us; the launch traced here: 425 us
  local copies, waits for them, and re-layouts  149 us (35%)
  waiting for transfers between devices  127 us (30%)
  blocking collectives  72.5 us (17%)
  matrix products  26.3 us (6%)
  other arithmetic  18.4 us (4%)
  starting transfers between devices  16.8 us (4%)
  between operations  14.7 us (3%)
    unnamed x27, local copies, waits for them, and re-layouts  84.2 us
    psum x1, waiting for transfers between devices, on_device(): summed = lax.psum(harmonic_amplitudes, 'lev')  74 us
    all_to_all x1, blocking collectives, on_device(): lax.all_to_all(scaled, 'wave', split_axis=0, concat_axis=3, tiled=True)  50.2 us
    all_to_all x1, waiting for transfers between devices, on_device(): lax.all_to_all(synthesis, 'wave', split_axis=3, concat_axis=0, tiled=True)  35.5 us
    all_to_all x3, local copies, waits for them, and re-layouts, on_device(): lax.all_to_all(synthesis, 'wave', split_axis=3, concat_axis=0, tiled=True)  25.7 us
    all_to_all x1, blocking collectives, on_device(): lax.all_to_all(quarter, 'lev', split_axis=2, concat_axis=3, tiled=True)  22.3 us
    all_to_all x3, local copies, waits for them, and re-layouts, on_device(): lax.all_to_all(scaled, 'wave', split_axis=0, concat_axis=3, tiled=True)  18 us
    all_to_all x1, waiting for transfers between devices, on_device(): lax.all_to_all(columns, 'lev', split_axis=3, concat_axis=2, tiled=True)  17.4 us
  transfers between devices with their start and end apart: 3, of which 3 were waited for; matrix products, arithmetic and copies ran while one was open for 0% of the time, Pallas kernels for 0%

commit v1 on v0

v1 whole, which is shorter than its diff:
```python
import functools

import jax
import jax.numpy as jnp
import numpy as np
from jax import lax
from jax.experimental import pallas as pl
from jax.experimental.pallas import tpu as pltpu
from jax.sharding import PartitionSpec as P

MESH = pl.DeviceIdType.MESH
LANES = 128


def kernel(
    dims,
    fourier,
    legendre,
    weights,
    points,
    zonal,
    zonal_row,
    balance,
    modes,
    project,
    eigen,
    reply,
    pick_div,
    pick_temp,
    place_div,
    place_temp,
    spectral,
    fourier_new,
    leg_full,
    leg_hi,
    leg_lo,
    mask_weight,
    mask_present,
    square,
    out_rows,
    in_rows,
    relay_a,
    relay_b,
    blocks,
    planes,
    grid_hi,
    grid_lo,
    partial,
    sum_a,
    sum_b,
    sum_left,
    sum_right,
    modal_in,
    modal_out,
    solved,
    mixed,
    spec_hi,
    spec_lo,
    packed,
    returned,
    final_rows,
    leg_sem,
    wave_send,
    wave_recv,
    lev_send,
    lev_recv,
    relay_recv,
    sum_send,
    sum_recv,
    gather_send,
    gather_recv,
    local_sem,
):
    nw, nx, band, lev, total, quarter = dims
    per = LANES // band
    groups = 4 * lev // per
    unit = (nw // nx) * groups
    half_unit = unit // 2
    rows = 2 * nx * lev
    half_rows = rows // 2
    tiles_j = quarter // LANES
    tiles_n = total // LANES
    half_n = total // 2
    highest = lax.Precision.HIGHEST
    f32, bf16 = jnp.float32, jnp.bfloat16
    w = lax.axis_index("wave")
    x = lax.axis_index("lev")
    right, left, far = lax.rem(x + 1, nx), lax.rem(x + nx - 1, nx), lax.rem(x + 2, nx)

    def remote(src, dst, send, recv, to_w, to_x):
        return pltpu.make_async_remote_copy(
            src_ref=src,
            dst_ref=dst,
            send_sem=send,
            recv_sem=recv,
            device_id=(to_w, to_x),
            device_id_type=MESH,
        )

    def drain(ref, sem):
        pltpu.make_async_copy(ref, ref, sem).wait()

    leg_copies = [
        pltpu.make_async_copy(legendre.at[s], leg_full.at[s], leg_sem.at[s])
        for s in range(2)
    ]
    for copy in leg_copies:
        copy.start()

    barrier = pltpu.get_barrier_semaphore()

    @pl.loop(1, nw)
    def _(k):
        pl.semaphore_signal(
            barrier, inc=1, device_id=(lax.rem(w + k, nw), x), device_id_type=MESH
        )

    for k in range(1, nx):
        pl.semaphore_signal(
            barrier, inc=1, device_id=(w, lax.rem(x + k, nx)), device_id_type=MESH
        )

    twice = 2 * zonal_row[...]
    for j in range(band):
        here = twice < points[w * band + j]
        mask_weight[j : j + 1, :] = jnp.where(here, weights[w * band + j], 0.0)
        mask_present[j : j + 1, :] = jnp.where(here, 1.0, 0.0)

    def first_row(g):
        pair, r = g // 2, g % 2
        c, third = pair // (lev // per), pair % (lev // per)
        return pl.multiple_of(((2 * c + r) * lev + per * third) * band, 8)

    @pl.loop(0, groups)
    def _(g):
        block = fourier[pl.ds(first_row(g), per * band), :]
        block = (block.reshape(per, band, LANES) * mask_weight[...][None]).reshape(
            per * band, LANES
        )
        block = jnp.concatenate(
            [block, jnp.zeros((LANES - per * band, LANES), f32)], axis=0
        )
        out_rows[pl.ds(g, 2 * nw, stride=groups), :] = block.T

    pl.semaphore_wait(barrier, nw - 1 + nx - 1)

    def wave_exchange(s, kind, source, target):
        @pl.loop(1, nw)
        def _(k):
            to = lax.rem(w + k, nw)
            remote(
                source(to), target(w), wave_send.at[kind, s], wave_recv.at[kind, s], to, x
            ).start()

        pltpu.make_async_copy(source(w), target(w), wave_recv.at[kind, s]).start()

    def wave_in(s):
        wave_exchange(
            s,
            0,
            lambda to: out_rows.at[
                pl.ds(pl.multiple_of((2 * to + s) * groups, 8), groups), :
            ],
            lambda me: in_rows.at[s, pl.ds(pl.multiple_of(me * groups, 8), groups), :],
        )

    def wave_out(s):
        wave_exchange(
            s,
            1,
            lambda to: returned.at[s, pl.ds(pl.multiple_of(to * groups, 8), groups), :],
            lambda me: final_rows.at[s, pl.ds(pl.multiple_of(me * groups, 8), groups), :],
        )

    def span(q, start=0, size=unit):
        return pl.ds(pl.multiple_of(q * unit + start, 8), size)

    def lev_start(s, kind, source, target):
        send, recv = lev_send.at[kind, s], lev_recv.at[kind, s]
        remote(
            source.at[s, span(far, 0, half_unit), :],
            relay_a.at[kind, s],
            send,
            relay_recv.at[kind, s, 0],
            w,
            right,
        ).start()
        remote(
            source.at[s, span(far, half_unit, half_unit), :],
            relay_b.at[kind, s],
            send,
            relay_recv.at[kind, s, 1],
            w,
            left,
        ).start()
        for to in (right, left):
            remote(
                source.at[s, span(to), :], target.at[s, span(x), :], send, recv, w, to
            ).start()
        pltpu.make_async_copy(
            source.at[s, span(x), :], target.at[s, span(x), :], recv
        ).start()

    def lev_forward(s, kind, target):
        send, recv = lev_send.at[kind, s], lev_recv.at[kind, s]
        drain(relay_a.at[kind, s], relay_recv.at[kind, s, 0])
        remote(
            relay_a.at[kind, s],
            target.at[s, span(left, 0, half_unit), :],
            send,
            recv,
            w,
            right,
        ).start()
        drain(relay_b.at[kind, s], relay_recv.at[kind, s, 1])
        remote(
            relay_b.at[kind, s],
            target.at[s, span(right, half_unit, half_unit), :],
            send,
            recv,
            w,
            left,
        ).start()

    def lev_wait(s, kind, target):
        drain(target.at[s], lev_recv.at[kind, s])

    lane = lax.broadcasted_iota(jnp.int32, (groups, LANES), 1)

    def unpack(s):
        @pl.loop(0, nx)
        def _(lg):
            base = lg * unit
            bands = [
                blocks[s, pl.ds(pl.multiple_of(base + b * groups, 8), groups), :]
                for b in range(nw // nx)
            ]
            for i in range(per):
                at = pl.ds(pl.multiple_of((lg * per + i) * groups, 8), groups)
                for t in range(tiles_j):
                    value = None
                    for b in range(nw // nx):
                        low = b * band - t * LANES
                        if low + band <= 0 or low >= LANES:
                            continue
                        turn = (low - i * band) % LANES
                        moved = pltpu.roll(bands[b], turn, 1) if turn else bands[b]
                        value = moved if value is None else jnp.where(lane >= low, moved, value)
                    planes[t, at, :] = value
        for t in range(tiles_j):
            for r in range(2):
                value = planes[t, pl.ds(r, rows, stride=2), :]
                high = value.astype(bf16)
                grid_hi[r * rows : (r + 1) * rows, t * LANES : (t + 1) * LANES] = high
                grid_lo[r * rows : (r + 1) * rows, t * LANES : (t + 1) * LANES] = (
                    value - high.astype(f32)
                ).astype(bf16)

    def analysis(s, q):
        r, part = q // 2, q % 2
        at = pl.ds(pl.multiple_of(r * rows, 16), rows)
        a_hi, a_lo = grid_hi[at, :], grid_lo[at, :]
        n_at = pl.ds(pl.multiple_of(part * half_n, 16), half_n)
        b_hi, b_lo = leg_hi[s, n_at, :], leg_lo[s, n_at, :]
        dot = functools.partial(
            lax.dot_general,
            dimension_numbers=(((1,), (1,)), ((), ())),
            preferred_element_type=f32,
        )
        partial[s, q] = dot(a_hi, b_hi) + (dot(a_hi, b_lo) + dot(a_lo, b_hi))

    top, bottom = pl.ds(0, half_rows), pl.ds(half_rows, half_rows)

    def reduce_start(s):
        send = sum_send.at[s]
        analysis(s, far)
        remote(
            partial.at[s, far, top], sum_a.at[s], send, sum_recv.at[s, 0], w, right
        ).start()
        remote(
            partial.at[s, far, bottom], sum_b.at[s], send, sum_recv.at[s, 1], w, left
        ).start()
        analysis(s, right)
        remote(
            partial.at[s, right, bottom],
            sum_left.at[s, bottom],
            send,
            sum_recv.at[s, 2],
            w,
            right,
        ).start()
        analysis(s, left)
        remote(
            partial.at[s, left, top],
            sum_right.at[s, top],
            send,
            sum_recv.at[s, 3],
            w,
            left,
        ).start()
        analysis(s, x)

    def reduce_forward(s):
        send = sum_send.at[s]
        drain(sum_a.at[s], sum_recv.at[s, 0])
        partial[s, right, top, :] += sum_a[s]
        remote(
            partial.at[s, right, top],
            sum_left.at[s, top],
            send,
            sum_recv.at[s, 4],
            w,
            right,
        ).start()
        drain(sum_b.at[s], sum_recv.at[s, 1])
        partial[s, left, bottom, :] += sum_b[s]
        remote(
            partial.at[s, left, bottom],
            sum_right.at[s, bottom],
            send,
            sum_recv.at[s, 5],
            w,
            left,
        ).start()

    def solve(s):
        drain(sum_left.at[s, bottom], sum_recv.at[s, 2])
        drain(sum_right.at[s, top], sum_recv.at[s, 3])
        drain(sum_left.at[s, top], sum_recv.at[s, 4])
        drain(sum_right.at[s, bottom], sum_recv.at[s, 5])
        value = partial[s, x] + (sum_left[s] + sum_right[s])
        n = lax.broadcasted_iota(jnp.int32, (1, half_n), 1) + (x % 2) * half_n
        value = jnp.where(n >= zonal[2 * w + s], value, 0.0)
        factor = (n * (n + 1)).astype(f32) * (4.0 / (total * (total + 1)))
        size = nx * lev
        both = jnp.dot(modal_in[...], value, precision=highest, preferred_element_type=f32)
        diagonal = lax.broadcasted_iota(jnp.int32, (size, size), 0) == lax.broadcasted_iota(
            jnp.int32, (size, size), 1
        )
        depth = jnp.sum(jnp.where(diagonal, eigen[...], 0.0), axis=1, keepdims=True)
        modal = (both[:size] + factor * both[size:]) / (1.0 + depth * factor)
        answer = jnp.dot(modal_out[...], modal, precision=highest, preferred_element_type=f32)
        row = lax.broadcasted_iota(jnp.int32, (rows, 1), 0)
        thermal = (row // (lev // per)) % 2 == 1
        solved[s, x] = answer + jnp.where(thermal, value, 0.0)

    def gather_start(s):
        send = gather_send.at[s]
        for to, first in ((right, 0), (left, 1)):
            for part in (first, 1 - first):
                at = (top, bottom)[part]
                remote(
                    solved.at[s, x, at],
                    solved.at[s, x, at],
                    send,
                    gather_recv.at[s, 2 * first + part],
                    w,
                    to,
                ).start()

    def gather_forward(s):
        send = gather_send.at[s]
        drain(solved.at[s, left, top], gather_recv.at[s, 0])
        remote(
            solved.at[s, left, top],
            solved.at[s, left, top],
            send,
            gather_recv.at[s, 4],
            w,
            right,
        ).start()
        drain(solved.at[s, right, bottom], gather_recv.at[s, 3])
        remote(
            solved.at[s, right, bottom],
            solved.at[s, right, bottom],
            send,
            gather_recv.at[s, 5],
            w,
            left,
        ).start()

    def gather_wait(s):
        drain(solved.at[s, left, bottom], gather_recv.at[s, 1])
        drain(solved.at[s, right, top], gather_recv.at[s, 2])
        drain(solved.at[s, far, top], gather_recv.at[s, 4])
        drain(solved.at[s, far, bottom], gather_recv.at[s, 5])

    def synthesis(s):
        for r in range(2):
            for t in range(tiles_n):
                part, inner = t // (tiles_n // 2), t % (tiles_n // 2)
                mixed[t, pl.ds(r, rows, stride=2), :] = solved[
                    s, 2 * r + part, :, inner * LANES : (inner + 1) * LANES
                ]
        for t in range(tiles_n):
            value = mixed[t]
            high = value.astype(bf16)
            spec_hi[:, t * LANES : (t + 1) * LANES] = high
            spec_lo[:, t * LANES : (t + 1) * LANES] = (value - high.astype(f32)).astype(bf16)
        start = 0
        while start < quarter:
            size = min(256, quarter - start)
            b_hi = leg_hi[s, :, start : start + size]
            b_lo = leg_lo[s, :, start : start + size]
            dot = functools.partial(jnp.dot, preferred_element_type=f32)
            value = dot(spec_hi[...], b_hi) + (
                dot(spec_hi[...], b_lo) + dot(spec_lo[...], b_hi)
            )
            for t in range(size // LANES):
                planes[start // LANES + t] = value[:, t * LANES : (t + 1) * LANES]
            start += size

    def write_spectral(s):
        thirds = lev // per
        for t in range(tiles_n):
            for i in range(per):
                for c in range(2):
                    for r in range(2):
                        value = mixed[
                            t,
                            pl.ds(x * per * groups + groups * i + 2 * thirds * c + r, thirds, stride=2),
                            :,
                        ]
                        spectral[
                            s, t, pl.ds(4 * i + 2 * c + r, thirds, stride=4 * per), :
                        ] = value

    def pack(s):
        @pl.loop(0, nx)
        def _(lg):
            for b in range(nw // nx):
                value = None
                for i in range(per):
                    at = pl.ds(pl.multiple_of((lg * per + i) * groups, 8), groups)
                    t, low = (b * band) // LANES, (b * band) % LANES
                    turn = (i * band - low) % LANES
                    source = planes[t, at, :]
                    moved = pltpu.roll(source, turn, 1) if turn else source
                    if low + band > LANES:
                        other = planes[t + 1, at, :]
                        other = pltpu.roll(other, turn, 1) if turn else other
                        moved = jnp.where(lane >= i * band + LANES - low, other, moved)
                    value = moved if value is None else jnp.where(lane >= i * band, moved, value)
                packed[s, pl.ds(pl.multiple_of(lg * unit + b * groups, 8), groups), :] = value

    wave_in(0)
    wave_in(1)

    chunk = 64
    for s in range(2):
        leg_copies[s].wait()

        @pl.loop(0, total // chunk)
        def _(k):
            at = pl.ds(pl.multiple_of(k * chunk, chunk), chunk)
            value = leg_full[s, at, :]
            high = value.astype(bf16)
            leg_hi[s, at, :] = high
            leg_lo[s, at, :] = (value - high.astype(f32)).astype(bf16)

    exact = functools.partial(jnp.dot, precision=highest, preferred_element_type=f32)
    size = nx * lev
    modal_in[:size, :] = exact(project[...], pick_div[...])
    modal_in[size:, :] = exact(exact(project[...], balance[...]), pick_temp[...])
    modal_out[...] = exact(place_div[...], modes[...]) - exact(
        place_temp[...], exact(reply[...], modes[...])
    )

    drain(in_rows.at[0], wave_recv.at[0, 0])
    lev_start(0, 0, in_rows, blocks)
    lev_forward(0, 0, blocks)
    lev_wait(0, 0, blocks)
    unpack(0)
    reduce_start(0)
    drain(in_rows.at[1], wave_recv.at[0, 1])
    lev_start(1, 0, in_rows, blocks)
    reduce_forward(0)
    lev_forward(1, 0, blocks)
    solve(0)
    gather_start(0)
    lev_wait(1, 0, blocks)
    unpack(1)
    gather_forward(0)
    reduce_start(1)
    gather_wait(0)
    reduce_forward(1)
    synthesis(0)
    pack(0)
    lev_start(0, 1, packed, returned)
    solve(1)
    gather_start(1)
    lev_forward(0, 1, returned)
    write_spectral(0)
    gather_forward(1)
    lev_wait(0, 1, returned)
    wave_out(0)
    gather_wait(1)
    synthesis(1)
    pack(1)
    lev_start(1, 1, packed, returned)
    write_spectral(1)
    lev_forward(1, 1, returned)
    lev_wait(1, 1, returned)
    wave_out(1)

    sent = (nw - 1) * groups
    for s in range(2):
        for kind in range(2):
            drain(in_rows.at[s, pl.ds(0, sent), :], wave_send.at[kind, s])
            drain(blocks.at[s], lev_send.at[kind, s])
        drain(solved.at[s, pl.ds(0, 3)], sum_send.at[s])
        drain(solved.at[s, pl.ds(0, 3)], gather_send.at[s])
    for s in range(2):
        drain(final_rows.at[s], wave_recv.at[1, s])

    present = mask_present[...] > 0.5

    @pl.loop(0, groups)
    def _(g):
        for s in range(2):
            square[pl.ds(s, nw, stride=2), :] = final_rows[s, pl.ds(g, nw, stride=groups), :]
        block = square[...].T[: per * band].reshape(per, band, LANES)
        block = jnp.where(present[None], block, 0.0).reshape(per * band, LANES)
        fourier_new[pl.ds(first_row(g), per * band), :] = block


def on_device(
    nw,
    nx,
    fourier,
    legendre,
    weights,
    points,
    zonal,
    pressure_balance_matrix,
    modes,
    project,
    eigen,
    thermal_reply_matrix,
):
    waves, parts, lev, band = fourier.shape
    slots, total, quarter = legendre.shape
    size = nx * lev
    per = LANES // band
    groups = parts * lev // per
    unit = (nw // nx) * groups
    rows = 2 * size
    half_n = total // 2
    dims = (nw, nx, band, lev, total, quarter)

    pick = np.zeros((2, size, rows), np.float32)
    row = 0
    for group in range(nx):
        for i in range(per):
            for c in range(2):
                for third in range(lev // per):
                    pick[c, group * lev + per * third + i, row] = 1.0
                    row += 1

    view = fourier.transpose(1, 2, 3, 0).reshape(parts * lev * band, waves)
    f32, bf16 = jnp.float32, jnp.bfloat16
    vmem = pl.BlockSpec(memory_space=pltpu.VMEM)
    smem = pl.BlockSpec(memory_space=pltpu.SMEM)
    dma = pltpu.SemaphoreType.DMA
    spectral, fourier_new = pl.pallas_call(
        functools.partial(kernel, dims),
        out_shape=(
            jax.ShapeDtypeStruct((slots, total // LANES, parts * lev, LANES), f32),
            jax.ShapeDtypeStruct(view.shape, f32),
        ),
        in_specs=[vmem, pl.BlockSpec(memory_space=pl.ANY), smem, smem, smem] + [vmem] * 10,
        out_specs=(vmem, vmem),
        scratch_shapes=[
            pltpu.VMEM((slots, total, quarter), f32),
            pltpu.VMEM((slots, total, quarter), bf16),
            pltpu.VMEM((slots, total, quarter), bf16),
            pltpu.VMEM((band, LANES), f32),
            pltpu.VMEM((band, LANES), f32),
            pltpu.VMEM((LANES, LANES), f32),
            pltpu.VMEM((waves * groups, LANES), f32),
            pltpu.VMEM((slots, nw * groups, LANES), f32),
            pltpu.VMEM((2, slots, unit // 2, LANES), f32),
            pltpu.VMEM((2, slots, unit // 2, LANES), f32),
            pltpu.VMEM((slots, nx * unit, LANES), f32),
            pltpu.VMEM((quarter // LANES, 2 * rows, LANES), f32),
            pltpu.VMEM((2 * rows, quarter), bf16),
            pltpu.VMEM((2 * rows, quarter), bf16),
            pltpu.VMEM((slots, 4, rows, half_n), f32),
            pltpu.VMEM((slots, rows // 2, half_n), f32),
            pltpu.VMEM((slots, rows // 2, half_n), f32),
            pltpu.VMEM((slots, rows, half_n), f32),
            pltpu.VMEM((slots, rows, half_n), f32),
            pltpu.VMEM((rows, rows), f32),
            pltpu.VMEM((rows, size), f32),
            pltpu.VMEM((slots, 4, rows, half_n), f32),
            pltpu.VMEM((total // LANES, 2 * rows, LANES), f32),
            pltpu.VMEM((2 * rows, total), bf16),
            pltpu.VMEM((2 * rows, total), bf16),
            pltpu.VMEM((slots, nx * unit, LANES), f32),
            pltpu.VMEM((slots, nx * unit, LANES), f32),
            pltpu.VMEM((slots, nw * groups, LANES), f32),
            dma((2,)),
            dma((2, 2)),
            dma((2, 2)),
            dma((2, 2)),
            dma((2, 2)),
            dma((2, 2, 2)),
            dma((2,)),
            dma((2, 6)),
            dma((2,)),
            dma((2, 6)),
            dma((1,)),
        ],
        compiler_params=pltpu.CompilerParams(
            collective_id=0, has_side_effects=True, vmem_limit_bytes=58 * 1024 * 1024
        ),
    )(
        view,
        legendre,
        weights,
        points,
        zonal,
        zonal.reshape(1, waves),
        pressure_balance_matrix,
        modes,
        project,
        eigen.reshape(1, size),
        thermal_reply_matrix,
        jnp.asarray(pick[0]),
        jnp.asarray(pick[1]),
        jnp.asarray(pick[0].T),
        jnp.asarray(pick[1].T),
    )
    spectral = (
        spectral.reshape(slots, total // LANES, lev, parts, LANES)
        .transpose(0, 3, 2, 1, 4)
        .reshape(slots, parts, lev, total)
    )
    fourier_new = fourier_new.reshape(parts, lev, band, waves).transpose(3, 0, 1, 2)
    return (spectral, fourier_new)


def solution(mesh):
    return jax.shard_map(
        functools.partial(on_device, mesh.shape["wave"], mesh.shape["lev"]),
        mesh=mesh,
        in_specs=(
            P(None, None, "lev", "wave"),
            P("wave", None, "lev"),
            P(),
            P(),
            P(),
            P(),
            P(),
            P(),
            P(),
            P(),
        ),
        out_specs=(P("wave", None, "lev", None), P(None, None, "lev", "wave")),
        check_vma=False,
    )
```

time: 430 us -> 155 us (0.36); the launches traced: 425 us -> 155 us
  Pallas kernels: 0 us -> 151 us
  local copies, waits for them, and re-layouts: 149 us -> 3.68 us
  waiting for transfers between devices: 127 us -> 0 us
  blocking collectives: 72.5 us -> 0 us
  matrix products: 26.3 us -> 0 us
  other arithmetic: 18.4 us -> 0 us
  starting transfers between devices: 16.8 us -> 0 us
  between operations: 14.7 us -> 0.65 us
    pallas_call x0 -> x1, Pallas kernels: none -> 151 us  [on_device(): pl.pallas_call(functools.partial(kernel, dims), out_shape=(jax.ShapeDtype...]
    unnamed x27 -> x3, local copies, waits for them, and re-layouts: 84.2 us -> 1.11 us
    psum x1 -> x0, waiting for transfers between devices: 74 us -> none  [on_device(): summed = lax.psum(harmonic_amplitudes, 'lev')]
    all_to_all x2 -> x0, blocking collectives: 72.5 us -> none  [the longest x1 50.2 us: on_device(): lax.all_to_all(scaled, 'wave', split_axis=0, concat_axis=3, tiled=True)]
    all_to_all x8 -> x0, local copies, waits for them, and re-layouts: 59.6 us -> none  [the longest x3 25.7 us: on_device(): lax.all_to_all(synthesis, 'wave', split_axis=3, concat_axis=0, tiled=True)]
    all_to_all x2 -> x0, waiting for transfers between devices: 52.9 us -> none  [the longest x1 35.5 us: on_device(): lax.all_to_all(synthesis, 'wave', split_axis=3, concat_axis=0, tiled=True)]
    dot_general x6 -> x0, matrix products: 26.3 us -> none  [the longest x1 10.6 us: on_device(): jnp.einsum('mclj,mnj->mcln', blocks, legendre, precision=highest)]
    all_to_all x2 -> x0, starting transfers between devices: 16.3 us -> none  [the longest x1 12.2 us: on_device(): lax.all_to_all(synthesis, 'wave', split_axis=3, concat_axis=0, tiled=True)]
  transfers between devices with their start and end apart: 3 -> 0, of which waited for: 3 -> 0; matrix products, arithmetic and copies ran while one was open for 0% -> 0% of each run, Pallas kernels for 0% -> 0%
where the time goes in v1:
time: 155 us
  Pallas kernels  151 us (97%)
  local copies, waits for them, and re-layouts  3.68 us (2%)
    pallas_call x1, Pallas kernels, on_device(): pl.pallas_call(functools.partial(kernel, dims), out_shape=(jax.ShapeDtype...  151 us

profile of v1, /device:TPU:1, one launch (start us, length us, event | category | flops | bytes accessed | tf_op | source)
XLA Modules:
  0.0 155.1 jit_solution(1621318762866650421)
XLA Ops:
  0.6 150.8 %shard_map.149 = (f32[2,10,72,128]{3,2,1,0:T(8,128)}, f32[2880,128]{1,0:T(8,128)}) custom-call(f32[2880,128]{1,0:T(8,128)} %bitcast.15, f32[2,1280,640]{2,1,0:T(8,128)} %legendre.1, f32[2560]{0:T(1024)} %weights.1, s32[2560]{0:T(1024)} %points.1, s32[128]{0:T(128)} %zonal.1, s32[1,128]{1,0:T(1,128)} %bitcast.18, f32[72,72]{1,0:T(8,128)} %balance.1, ...), custom_call_target="tpu_custom_call" | custom-call | tf_op jit(solution)/shard_map/pallas_call | solution.py:565
  151.4 0.0 copy-start
  151.5 1.4 copy.19
  152.9 1.1 reshape.26
  154.0 0.0 copy-done
  154.0 1.1 copy.21
Async XLA Ops:
  151.4 2.6 %copy-start = (f32[2880,128]{1,0:T(8,128)S(1)}, f32[2880,128]{1,0:T(8,128)}, u32[]{:S(2)}) copy-start(f32[2880,128]{1,0:T(8,128)} %get-tuple-element.5) | copy-start | bytes 4423684

commit v2 on v1

v2 whole, which is shorter than its diff:
```python
import functools

import jax
import jax.numpy as jnp
import numpy as np
from jax import lax
from jax.experimental import pallas as pl
from jax.experimental.pallas import tpu as pltpu
from jax.sharding import PartitionSpec as P

MESH = pl.DeviceIdType.MESH
LANES = 128
CHUNKS_IN = (((0, 8), (8, 8), (16, 8)), ((0, 8), (8, 8), (16, 8)))
CHUNKS_OUT = (((0, 8), (8, 8), (16, 8)), ((0, 8), (8, 8), (16, 8)))


def kernel(
    dims,
    fourier,
    legendre,
    weights,
    points,
    zonal,
    zonal_row,
    balance,
    modes,
    project,
    eigen,
    reply,
    pick_div,
    pick_temp,
    place_div,
    place_temp,
    spectral,
    fourier_new,
    leg_full,
    leg_hi,
    leg_lo,
    mask_weight,
    mask_present,
    square,
    out_rows,
    in_rows,
    blocks,
    planes_in,
    planes_out,
    grid_hi,
    grid_lo,
    partial,
    sum_a,
    sum_b,
    sum_left,
    sum_right,
    modal_in,
    modal_out,
    solved,
    mixed,
    spec_hi,
    spec_lo,
    spec_rows,
    packed,
    returned,
    final,
    result,
    leg_sem,
    wave_send,
    wave_recv,
    lev_send,
    lev_recv,
    sum_send,
    sum_recv,
    gather_send,
    gather_recv,
    out_sem,
):
    nw, nx, band, lev, total, quarter = dims
    per = LANES // band
    thirds = lev // per
    pairs = 2 * thirds
    cells = nx * per
    groups = 2 * pairs
    near = nw // nx
    size = nx * lev
    rows = 2 * size
    tiles_j = quarter // LANES
    tiles_n = total // LANES
    half_n = total // 2
    half = LANES // 2
    whole = 2 * rows + size
    highest = lax.Precision.HIGHEST
    f32, bf16 = jnp.float32, jnp.bfloat16
    w = lax.axis_index("wave")
    x = lax.axis_index("lev")
    right, left, far = lax.rem(x + 1, nx), lax.rem(x + nx - 1, nx), lax.rem(x + 2, nx)
    chunks = (CHUNKS_IN, CHUNKS_OUT)

    def remote(src, dst, send, recv, to_w, to_x):
        return pltpu.make_async_remote_copy(
            src_ref=src,
            dst_ref=dst,
            send_sem=send,
            recv_sem=recv,
            device_id=(to_w, to_x),
            device_id_type=MESH,
        )

    def drain(ref, sem):
        pltpu.make_async_copy(ref, ref, sem).wait()

    leg_copies = [
        pltpu.make_async_copy(legendre.at[s], leg_full.at[s], leg_sem.at[s])
        for s in range(2)
    ]
    for copy in leg_copies:
        copy.start()

    barrier = pltpu.get_barrier_semaphore()

    @pl.loop(1, nw)
    def _(k):
        pl.semaphore_signal(
            barrier, inc=1, device_id=(lax.rem(w + k, nw), x), device_id_type=MESH
        )

    for k in range(1, nx):
        pl.semaphore_signal(
            barrier, inc=1, device_id=(w, lax.rem(x + k, nx)), device_id_type=MESH
        )

    twice = 2 * zonal_row[...]
    for j in range(band):
        here = twice < points[w * band + j]
        mask_weight[j : j + 1, :] = jnp.where(here, weights[w * band + j], 0.0)
        mask_present[j : j + 1, :] = jnp.where(here, 1.0, 0.0)

    def first_row(r, k):
        c, third = k // thirds, k % thirds
        return pl.multiple_of(((2 * c + r) * lev + per * third) * band, 8)

    def spread(r):
        @pl.loop(0, pairs)
        def _(k):
            block = fourier[pl.ds(first_row(r, k), per * band), :]
            block = (block.reshape(per, band, LANES) * mask_weight[...][None]).reshape(
                per * band, LANES
            )
            block = jnp.concatenate(
                [block, jnp.zeros((LANES - per * band, LANES), f32)], axis=0
            )
            out_rows[r, pl.ds(k, 2 * nw, stride=pairs), :] = block.T

    def from_wave(index, chunk):
        first, n = chunk
        return pl.ds(pl.multiple_of(nw * first + index * n, 8), n)

    def all_waves(chunk, count=nw):
        first, n = chunk
        return pl.ds(nw * first, count * n)

    def wave_exchange(kind, r, c, source, target):
        send, recv = wave_send.at[kind, r, c], wave_recv.at[kind, r, c]

        @pl.loop(1, nw)
        def _(k):
            to = lax.rem(w + k, nw)
            remote(source(to), target, send, recv, to, x).start()

        pltpu.make_async_copy(source(w), target, recv).start()

    def wave_in(r, c):
        chunk = chunks[0][r][c]
        first, n = chunk
        wave_exchange(
            0,
            r,
            c,
            lambda to: out_rows.at[r, pl.ds(pl.multiple_of(to * groups + first, 8), n), :],
            in_rows.at[r, from_wave(w, chunk), :],
        )

    def wave_in_wait(r, c):
        drain(in_rows.at[r, all_waves(chunks[0][r][c]), :], wave_recv.at[0, r, c])

    def wave_out(r, c):
        chunk = chunks[1][r][c]
        wave_exchange(
            1,
            r,
            c,
            lambda to: returned.at[r, from_wave(to, chunk), :],
            final.at[r, from_wave(w, chunk), :],
        )

    def wave_out_wait(r, c):
        drain(final.at[r, all_waves(chunks[1][r][c]), :], wave_recv.at[1, r, c])

    def span(q, chunk):
        first, n = chunk
        return pl.ds(pl.multiple_of(nw * first + q * (near * n), 8), near * n)

    def lev_start(kind, r, c):
        source, target = ((in_rows, blocks), (packed, returned))[kind]
        chunk = chunks[kind][r][c]
        send, recv = lev_send.at[kind, r, c], lev_recv.at[kind, r, c]
        for to in (far, right, left):
            remote(
                source.at[r, span(to, chunk), :],
                target.at[r, span(x, chunk), :],
                send,
                recv,
                w,
                to,
            ).start()
        pltpu.make_async_copy(
            source.at[r, span(x, chunk), :], target.at[r, span(x, chunk), :], recv
        ).start()

    def lev_wait(kind, r, c):
        target = (blocks, returned)[kind]
        drain(target.at[r, all_waves(chunks[kind][r][c]), :], lev_recv.at[kind, r, c])

    def unpack(r, c):
        chunk = chunks[0][r][c]
        first, n = chunk
        lane = lax.broadcasted_iota(jnp.int32, (n, LANES), 1)

        @pl.loop(0, nx)
        def _(lg):
            bands = [
                blocks[r, from_wave(lg * near + b, chunk), :]
                for b in range(near)
            ]
            for i in range(per):
                at = pl.ds(first * cells + lg * per + i, n, stride=cells)
                for t in range(tiles_j):
                    value = None
                    for b in range(near):
                        low = b * band - t * LANES
                        if low + band <= 0 or low >= LANES:
                            continue
                        turn = (low - i * band) % LANES
                        moved = pltpu.roll(bands[b], turn, 1) if turn else bands[b]
                        value = moved if value is None else jnp.where(lane >= low, moved, value)
                    planes_in[t, at, :] = value

    def analysis(p, h):
        s = p % 2
        n_at = pl.ds(pl.multiple_of(h * half_n, 16), half_n)
        b_hi, b_lo = leg_hi[s, n_at, :], leg_lo[s, n_at, :]
        dot = functools.partial(
            lax.dot_general,
            dimension_numbers=(((1,), (1,)), ((), ())),
            preferred_element_type=f32,
        )
        value = dot(grid_hi[...], b_hi) + (
            dot(grid_hi[...], b_lo) + dot(grid_lo[...], b_hi)
        )
        low = lax.broadcasted_iota(jnp.int32, (size, LANES), 1) < half
        even, odd = 2 * h, 2 * h + 1
        partial[p, even, 0:rows, :] = value[:, 0:LANES]
        partial[p, even, rows : 2 * rows, :] = value[:, LANES : 2 * LANES]
        middle = value[:, 2 * LANES : 3 * LANES]
        first, second = middle[:size], middle[size:]
        partial[p, even, 2 * rows :, :] = jnp.where(low, first, pltpu.roll(second, half, 1))
        partial[p, odd, 2 * rows :, :] = jnp.where(low, pltpu.roll(first, half, 1), second)
        partial[p, odd, 0:rows, :] = value[:, 3 * LANES : 4 * LANES]
        partial[p, odd, rows : 2 * rows, :] = value[:, 4 * LANES : 5 * LANES]

    cut = (whole // 2 + 7) // 8 * 8
    top, bottom = pl.ds(0, cut), pl.ds(cut, whole - cut)

    def reduce_start(p):
        r, s = p // 2, p % 2
        for t in range(tiles_j):
            value = planes_in[t, s * rows : (s + 1) * rows, :]
            high = value.astype(bf16)
            grid_hi[:, t * LANES : (t + 1) * LANES] = high
            grid_lo[:, t * LANES : (t + 1) * LANES] = (value - high.astype(f32)).astype(bf16)
        send = sum_send.at[p]
        analysis(p, far // 2)
        remote(
            partial.at[p, far, top], sum_a.at[p], send, sum_recv.at[p, 0], w, right
        ).start()
        remote(
            partial.at[p, far, bottom], sum_b.at[p], send, sum_recv.at[p, 1], w, left
        ).start()
        analysis(p, x // 2)
        remote(
            partial.at[p, right, bottom],
            sum_left.at[p, bottom],
            send,
            sum_recv.at[p, 2],
            w,
            right,
        ).start()
        remote(
            partial.at[p, left, top],
            sum_right.at[p, top],
            send,
            sum_recv.at[p, 3],
            w,
            left,
        ).start()

    def reduce_forward(p):
        send = sum_send.at[p]
        drain(sum_a.at[p], sum_recv.at[p, 0])
        partial[p, right, top, :] += sum_a[p]
        remote(
            partial.at[p, right, top],
            sum_left.at[p, top],
            send,
            sum_recv.at[p, 4],
            w,
            right,
        ).start()
        drain(sum_b.at[p], sum_recv.at[p, 1])
        partial[p, left, bottom, :] += sum_b[p]
        remote(
            partial.at[p, left, bottom],
            sum_right.at[p, bottom],
            send,
            sum_recv.at[p, 5],
            w,
            left,
        ).start()

    def solve(p):
        s = p % 2
        drain(sum_left.at[p, bottom], sum_recv.at[p, 2])
        drain(sum_right.at[p, top], sum_recv.at[p, 3])
        drain(sum_left.at[p, top], sum_recv.at[p, 4])
        drain(sum_right.at[p, bottom], sum_recv.at[p, 5])
        value = partial[p, x] + (sum_left[p] + sum_right[p])
        lanes = lax.broadcasted_iota(jnp.int32, (1, LANES), 1)
        start, odd = (x // 2) * half_n, x % 2
        first = start + odd * (half_n - 2 * LANES) + lanes
        middle = start + 2 * LANES + odd * half + lanes % half
        n = jnp.concatenate([first, first + LANES, middle], axis=1)
        mixed_part = value[2 * rows :]
        value = jnp.concatenate(
            [
                value[:rows],
                value[rows : 2 * rows],
                jnp.concatenate([mixed_part, pltpu.roll(mixed_part, half, 1)], axis=0),
            ],
            axis=1,
        )
        value = jnp.where(n >= zonal[2 * w + s], value, 0.0)
        factor = (n * (n + 1)).astype(f32) * (4.0 / (total * (total + 1)))
        both = jnp.dot(modal_in[...], value, precision=highest, preferred_element_type=f32)
        diagonal = lax.broadcasted_iota(jnp.int32, (size, size), 0) == lax.broadcasted_iota(
            jnp.int32, (size, size), 1
        )
        depth = jnp.sum(jnp.where(diagonal, eigen[...], 0.0), axis=1, keepdims=True)
        modal = (both[:size] + factor * both[size:]) / (1.0 + depth * factor)
        answer = jnp.dot(modal_out[...], modal, precision=highest, preferred_element_type=f32)
        thermal = lax.broadcasted_iota(jnp.int32, (rows, 1), 0) >= size
        answer = answer + jnp.where(thermal, value, 0.0)
        solved[p, x, 0:rows, :] = answer[:, :LANES]
        solved[p, x, rows : 2 * rows, :] = answer[:, LANES : 2 * LANES]
        last = answer[:, 2 * LANES :]
        low = lax.broadcasted_iota(jnp.int32, (size, LANES), 1) < half
        solved[p, x, 2 * rows :, :] = jnp.where(
            low, last[:size], pltpu.roll(last[size:], half, 1)
        )

    def gather_start(p):
        send = gather_send.at[p]
        for step in range(2):
            for to, first in ((right, 0), (left, 1)):
                part = (first, 1 - first)[step]
                at = (top, bottom)[part]
                remote(
                    solved.at[p, x, at],
                    solved.at[p, x, at],
                    send,
                    gather_recv.at[p, 2 * first + part],
                    w,
                    to,
                ).start()

    def gather_forward(p):
        send = gather_send.at[p]
        drain(solved.at[p, left, top], gather_recv.at[p, 0])
        remote(
            solved.at[p, left, top],
            solved.at[p, left, top],
            send,
            gather_recv.at[p, 4],
            w,
            right,
        ).start()
        drain(solved.at[p, right, bottom], gather_recv.at[p, 3])
        remote(
            solved.at[p, right, bottom],
            solved.at[p, right, bottom],
            send,
            gather_recv.at[p, 5],
            w,
            left,
        ).start()

    def gather_wait(p):
        drain(solved.at[p, left, bottom], gather_recv.at[p, 1])
        drain(solved.at[p, right, top], gather_recv.at[p, 2])
        drain(solved.at[p, far, top], gather_recv.at[p, 4])
        drain(solved.at[p, far, bottom], gather_recv.at[p, 5])

    def synthesis(p):
        s = p % 2
        low = lax.broadcasted_iota(jnp.int32, (size, LANES), 1) < half
        for h in range(2):
            even, odd, t = 2 * h, 2 * h + 1, h * (tiles_n // 2)
            mixed[t] = solved[p, even, 0:rows, :]
            mixed[t + 1] = solved[p, even, rows : 2 * rows, :]
            before, after = solved[p, even, 2 * rows :, :], solved[p, odd, 2 * rows :, :]
            mixed[t + 2, 0:size, :] = jnp.where(low, before, pltpu.roll(after, half, 1))
            mixed[t + 2, size:, :] = jnp.where(low, pltpu.roll(before, half, 1), after)
            mixed[t + 3] = solved[p, odd, 0:rows, :]
            mixed[t + 4] = solved[p, odd, rows : 2 * rows, :]
        for t in range(tiles_n):
            value = mixed[t]
            high = value.astype(bf16)
            spec_hi[:, t * LANES : (t + 1) * LANES] = high
            spec_lo[:, t * LANES : (t + 1) * LANES] = (value - high.astype(f32)).astype(bf16)
        start = 0
        while start < quarter:
            width = min(256, quarter - start)
            b_hi = leg_hi[s, :, start : start + width]
            b_lo = leg_lo[s, :, start : start + width]
            dot = functools.partial(jnp.dot, preferred_element_type=f32)
            value = dot(spec_hi[...], b_hi) + (
                dot(spec_hi[...], b_lo) + dot(spec_lo[...], b_hi)
            )
            for t in range(width // LANES):
                planes_out[start // LANES + t, s * rows : (s + 1) * rows, :] = value[
                    :, t * LANES : (t + 1) * LANES
                ]
            start += width

    def write_spectral(p):
        r, s = p // 2, p % 2
        for t in range(tiles_n):
            for i in range(per):
                for c in range(2):
                    for third in range(thirds):
                        spec_rows[
                            s,
                            per * third + i,
                            2 * c + r : 2 * c + r + 1,
                            t * LANES : (t + 1) * LANES,
                        ] = mixed[t, pl.ds(c * size + third * cells + x * per + i, 1), :]

    def pack(r, c):
        chunk = chunks[1][r][c]
        first, n = chunk
        lane = lax.broadcasted_iota(jnp.int32, (n, LANES), 1)

        @pl.loop(0, nx)
        def _(lg):
            tiles = [
                [
                    planes_out[t, pl.ds(first * cells + lg * per + i, n, stride=cells), :]
                    for t in range(tiles_j)
                ]
                for i in range(per)
            ]
            for b in range(near):
                value = None
                for i in range(per):
                    t, low = (b * band) // LANES, (b * band) % LANES
                    turn = (i * band - low) % LANES
                    moved = tiles[i][t]
                    moved = pltpu.roll(moved, turn, 1) if turn else moved
                    if low + band > LANES:
                        other = tiles[i][t + 1]
                        other = pltpu.roll(other, turn, 1) if turn else other
                        moved = jnp.where(lane >= i * band + LANES - low, other, moved)
                    value = moved if value is None else jnp.where(lane >= i * band, moved, value)
                packed[r, from_wave(lg * near + b, chunk), :] = value

    def collect(r):
        present = mask_present[...] > 0.5
        for k in range(pairs):
            for s in range(2):
                at = s * pairs + k
                first, n = next(chunk for chunk in chunks[1][r] if at < sum(chunk))
                square[k % 2, pl.ds(s, nw, stride=2), :] = final[
                    r, pl.ds(nw * first + at - first, nw, stride=n), :
                ]
            block = square[k % 2].T[: per * band].reshape(per, band, LANES)
            block = jnp.where(present[None], block, 0.0).reshape(per * band, LANES)
            result[pl.ds(first_row(r, k), per * band), :] = block

    def write_back(r):
        for c in range(2):
            at = pl.ds((2 * c + r) * lev * band, lev * band)
            pltpu.make_async_copy(
                result.at[at, :], fourier_new.at[at, :], out_sem.at[r, c]
            ).start()

    def write_back_wait(r):
        for c in range(2):
            at = pl.ds((2 * c + r) * lev * band, lev * band)
            pltpu.make_async_copy(
                result.at[at, :], fourier_new.at[at, :], out_sem.at[r, c]
            ).wait()

    def split(s):
        leg_copies[s].wait()
        chunk = 64

        @pl.loop(0, total // chunk)
        def _(k):
            at = pl.ds(pl.multiple_of(k * chunk, chunk), chunk)
            value = leg_full[s, at, :]
            high = value.astype(bf16)
            leg_hi[s, at, :] = high
            leg_lo[s, at, :] = (value - high.astype(f32)).astype(bf16)

    def matrices():
        exact = functools.partial(jnp.dot, precision=highest, preferred_element_type=f32)
        modal_in[:size, :] = exact(project[...], pick_div[...])
        modal_in[size:, :] = exact(exact(project[...], balance[...]), pick_temp[...])
        modal_out[...] = exact(place_div[...], modes[...]) - exact(
            place_temp[...], exact(reply[...], modes[...])
        )

    spread(0)
    pl.semaphore_wait(barrier, nw - 1 + nx - 1)
    wave_in(0, 1)
    wave_in(0, 0)
    spread(1)
    wave_in(0, 2)
    wave_in_wait(0, 1)
    lev_start(0, 0, 1)
    lev_wait(0, 0, 1)
    split(0)
    unpack(0, 1)
    matrices()
    wave_in_wait(0, 0)
    lev_start(0, 0, 0)
    wave_in(1, 0)
    wave_in_wait(0, 2)
    lev_start(0, 0, 2)
    lev_wait(0, 0, 0)
    unpack(0, 0)
    reduce_start(0)
    wave_in(1, 1)
    lev_wait(0, 0, 2)
    wave_in_wait(1, 0)
    lev_start(0, 1, 0)
    reduce_forward(0)
    split(1)
    wave_in(1, 2)
    unpack(0, 2)
    reduce_start(1)
    solve(0)
    wave_in_wait(1, 1)
    gather_start(0)
    reduce_forward(1)
    lev_start(0, 1, 1)
    gather_forward(0)
    wave_in_wait(1, 2)
    solve(1)
    lev_wait(0, 1, 0)
    lev_start(0, 1, 2)
    gather_start(1)
    gather_wait(0)
    lev_wait(0, 1, 1)
    synthesis(0)
    unpack(1, 0)
    unpack(1, 1)
    reduce_start(2)
    write_spectral(0)
    gather_forward(1)
    pack(0, 0)
    lev_wait(0, 1, 2)
    reduce_forward(2)
    unpack(1, 2)
    lev_start(1, 0, 0)
    gather_wait(1)
    reduce_start(3)
    synthesis(1)
    solve(2)
    pack(0, 2)
    lev_start(1, 0, 2)
    pack(0, 1)
    lev_wait(1, 0, 0)
    reduce_forward(3)
    gather_start(2)
    lev_wait(1, 0, 2)
    lev_start(1, 0, 1)
    wave_out(0, 0)
    gather_forward(2)
    solve(3)
    gather_start(3)
    wave_out(0, 2)
    lev_wait(1, 0, 1)
    wave_out(0, 1)
    gather_wait(2)
    write_spectral(1)
    synthesis(2)
    gather_forward(3)
    pack(1, 0)
    write_spectral(2)
    lev_start(1, 1, 0)
    gather_wait(3)
    wave_out_wait(0, 2)
    synthesis(3)
    write_spectral(3)
    pack(1, 1)
    lev_start(1, 1, 1)
    wave_out_wait(0, 0)
    lev_wait(1, 1, 0)
    wave_out(1, 0)
    pack(1, 2)
    lev_wait(1, 1, 1)
    wave_out_wait(0, 1)
    lev_start(1, 1, 2)
    collect(0)
    spec_copy = pltpu.make_async_copy(spec_rows, spectral, out_sem.at[0, 2])
    spec_copy.start()
    wave_out(1, 1)
    lev_wait(1, 1, 2)
    write_back(0)
    wave_out(1, 2)

    for kind in range(2):
        for r in range(2):
            for c, chunk in enumerate(chunks[kind][r]):
                drain(in_rows.at[r, all_waves(chunk, nw - 1), :], wave_send.at[kind, r, c])
                sent = nw - near
                drain(in_rows.at[r, all_waves(chunk, sent), :], lev_send.at[kind, r, c])
    for p in range(4):
        drain(solved.at[p, pl.ds(0, 3)], sum_send.at[p])
        drain(solved.at[p, pl.ds(0, 3)], gather_send.at[p])
    for c in range(len(chunks[1][1])):
        wave_out_wait(1, c)
    collect(1)
    write_back(1)
    spec_copy.wait()
    write_back_wait(0)
    write_back_wait(1)


def on_device(
    nw,
    nx,
    fourier,
    legendre,
    weights,
    points,
    zonal,
    pressure_balance_matrix,
    modes,
    project,
    eigen,
    thermal_reply_matrix,
):
    waves, parts, lev, band = fourier.shape
    slots, total, quarter = legendre.shape
    size = nx * lev
    per = LANES // band
    groups = parts * lev // per
    rows = 2 * size
    whole = 2 * rows + size
    cut = (whole // 2 + 7) // 8 * 8
    tiles_n = total // LANES
    dims = (nw, nx, band, lev, total, quarter)

    pick = np.zeros((2, size, rows), np.float32)
    row = 0
    for c in range(2):
        for third in range(lev // per):
            for group in range(nx):
                for i in range(per):
                    pick[c, group * lev + per * third + i, row] = 1.0
                    row += 1

    view = fourier.transpose(1, 2, 3, 0).reshape(parts * lev * band, waves)
    f32, bf16 = jnp.float32, jnp.bfloat16
    vmem = pl.BlockSpec(memory_space=pltpu.VMEM)
    smem = pl.BlockSpec(memory_space=pltpu.SMEM)
    anywhere = pl.BlockSpec(memory_space=pl.ANY)
    dma = pltpu.SemaphoreType.DMA
    lines = pltpu.VMEM((2, nw * groups, LANES), f32)
    spectral, fourier_new = pl.pallas_call(
        functools.partial(kernel, dims),
        out_shape=(
            jax.ShapeDtypeStruct((slots, lev, parts, total), f32),
            jax.ShapeDtypeStruct(view.shape, f32),
        ),
        in_specs=[vmem, anywhere, smem, smem, smem] + [vmem] * 10,
        out_specs=(anywhere, anywhere),
        scratch_shapes=[
            pltpu.VMEM((slots, total, quarter), f32),
            pltpu.VMEM((slots, total, quarter), bf16),
            pltpu.VMEM((slots, total, quarter), bf16),
            pltpu.VMEM((band, LANES), f32),
            pltpu.VMEM((band, LANES), f32),
            pltpu.VMEM((2, LANES, LANES), f32),
            lines,
            lines,
            lines,
            pltpu.VMEM((quarter // LANES, 2 * rows, LANES), f32),
            pltpu.VMEM((quarter // LANES, 2 * rows, LANES), f32),
            pltpu.VMEM((rows, quarter), bf16),
            pltpu.VMEM((rows, quarter), bf16),
            pltpu.VMEM((4, nx, whole, LANES), f32),
            pltpu.VMEM((4, cut, LANES), f32),
            pltpu.VMEM((4, whole - cut, LANES), f32),
            pltpu.VMEM((4, whole, LANES), f32),
            pltpu.VMEM((4, whole, LANES), f32),
            pltpu.VMEM((rows, rows), f32),
            pltpu.VMEM((rows, size), f32),
            pltpu.VMEM((4, nx, whole, LANES), f32),
            pltpu.VMEM((tiles_n, rows, LANES), f32),
            pltpu.VMEM((rows, total), bf16),
            pltpu.VMEM((rows, total), bf16),
            pltpu.VMEM((slots, lev, parts, total), f32),
            lines,
            lines,
            lines,
            pltpu.VMEM(view.shape, f32),
            dma((2,)),
            dma((2, 2, 3)),
            dma((2, 2, 3)),
            dma((2, 2, 3)),
            dma((2, 2, 3)),
            dma((4,)),
            dma((4, 6)),
            dma((4,)),
            dma((4, 6)),
            dma((2, 3)),
        ],
        compiler_params=pltpu.CompilerParams(
            collective_id=0, has_side_effects=True, vmem_limit_bytes=58 * 1024 * 1024
        ),
    )(
        view,
        legendre,
        weights,
        points,
        zonal,
        zonal.reshape(1, waves),
        pressure_balance_matrix,
        modes,
        project,
        eigen.reshape(1, size),
        thermal_reply_matrix,
        jnp.asarray(pick[0]),
        jnp.asarray(pick[1]),
        jnp.asarray(pick[0].T),
        jnp.asarray(pick[1].T),
    )
    spectral = spectral.transpose(0, 2, 1, 3)
    fourier_new = fourier_new.reshape(parts, lev, band, waves).transpose(3, 0, 1, 2)
    return (spectral, fourier_new)


def solution(mesh):
    return jax.shard_map(
        functools.partial(on_device, mesh.shape["wave"], mesh.shape["lev"]),
        mesh=mesh,
        in_specs=(
            P(None, None, "lev", "wave"),
            P("wave", None, "lev"),
            P(),
            P(),
            P(),
            P(),
            P(),
            P(),
            P(),
            P(),
        ),
        out_specs=(P("wave", None, "lev", None), P(None, None, "lev", "wave")),
        check_vma=False,
    )
```

time: 155 us -> 135 us (0.87)
  Pallas kernels: 151 us -> 131 us
    pallas_call x1, Pallas kernels: 151 us -> 131 us  [on_device(): pl.pallas_call(functools.partial(kernel, dims), out_shape=(jax.ShapeDtype...]
    reshape x2 -> x0, local copies, waits for them, and re-layouts: 2.56 us -> none  [the longest x1 1.42 us: on_device(): spectral.reshape(slots, total // LANES, lev, parts, LANES)]
    unnamed x3 -> x4, local copies, waits for them, and re-layouts: 1.11 us -> 3.25 us
where the time goes in v2:
time: 135 us
  Pallas kernels  131 us (97%)
  local copies, waits for them, and re-layouts  3.25 us (2%)
    pallas_call x1, Pallas kernels, on_device(): pl.pallas_call(functools.partial(kernel, dims), out_shape=(jax.ShapeDtype...  131 us
    unnamed x4, local copies, waits for them, and re-layouts  3.25 us

profile of v2, /device:TPU:1, one launch (start us, length us, event | category | flops | bytes accessed | tf_op | source)
XLA Modules:
  0.0 134.7 jit_solution(15021165239537603011)
XLA Ops:
  0.6 130.8 %shard_map.149 = (f32[2,18,4,1280]{3,2,1,0:T(4,128)}, f32[2880,128]{1,0:T(8,128)}) custom-call(f32[2880,128]{1,0:T(8,128)} %bitcast.9, f32[2,1280,640]{2,1,0:T(8,128)} %legendre.1, f32[2560]{0:T(1024)} %weights.1, s32[2560]{0:T(1024)} %points.1, s32[128]{0:T(128)} %zonal.1, s32[1,128]{1,0:T(1,128)} %bitcast.12, f32[72,72]{1,0:T(8,128)} %balance.1, ...), custom_call_target="tpu_custom_call" | custom-call | tf_op jit(solution)/shard_map/pallas_call | solution.py:689
  131.5 0.0 copy-start
  131.5 2.1 %copy.18 = f32[2,4,18,1280]{3,1,2,0:T(4,128)} copy(f32[2,4,18,1280]{3,1,2,0:T(4,128)} %bitcast.11) | data formatting | bytes 1474560
  133.6 0.0 copy-done
  133.6 1.1 copy.19
Async XLA Ops:
  131.5 2.2 %copy-start = (f32[2880,128]{1,0:T(8,128)S(1)}, f32[2880,128]{1,0:T(8,128)}, u32[]{:S(2)}) copy-start(f32[2880,128]{1,0:T(8,128)} %get-tuple-element.5) | copy-start | bytes 4423684

commit v3 on v2

v3 whole, which is shorter than its diff:
```python
import functools

import jax
import jax.numpy as jnp
import numpy as np
from jax import lax
from jax.experimental import pallas as pl
from jax.experimental.pallas import tpu as pltpu
from jax.sharding import PartitionSpec as P

MESH = pl.DeviceIdType.MESH
LANES = 128
CHUNKS_IN = (((0, 8), (8, 8), (16, 8)), ((0, 8), (8, 8), (16, 8)))
WHOLE, LONG_FIRST, SHORT_FIRST = ((0, 12),), ((0, 8), (8, 4)), ((0, 4), (4, 8))
PARTS_SUM = (LONG_FIRST, WHOLE, WHOLE, WHOLE)
PARTS_GATHER = (WHOLE, WHOLE, WHOLE, SHORT_FIRST)
CHUNKS_OUT = (((0, 8), (8, 8), (16, 8)), ((0, 8), (8, 8), (16, 8)))


def kernel(
    dims,
    fourier,
    legendre,
    weights_far,
    points_far,
    zonal_far,
    balance_far,
    modes_far,
    project_far,
    eigen_far,
    reply_far,
    pick_div_far,
    pick_temp_far,
    place_div_far,
    place_temp_far,
    spectral,
    fourier_new,
    weights,
    points,
    zonal,
    balance,
    modes,
    project,
    eigen,
    reply,
    pick_div,
    pick_temp,
    place_div,
    place_temp,
    field,
    leg_full,
    leg_hi,
    leg_lo,
    mask_weight,
    mask_present,
    square,
    out_rows,
    in_rows,
    blocks,
    planes_in,
    planes_out,
    grid_hi,
    grid_lo,
    partial,
    sum_a,
    sum_b,
    sum_left,
    sum_right,
    modal_in,
    modal_out,
    solved,
    mixed,
    spec_hi,
    spec_lo,
    spec_rows,
    packed,
    returned,
    final,
    result,
    small_sem,
    field_sem,
    leg_sem,
    wave_send,
    wave_recv,
    lev_send,
    lev_recv,
    sum_send,
    sum_recv,
    gather_send,
    gather_recv,
    out_sem,
):
    nw, nx, band, lev, total, quarter = dims
    per = LANES // band
    thirds = lev // per
    pairs = 2 * thirds
    cells = nx * per
    groups = 2 * pairs
    near = nw // nx
    size = nx * lev
    rows = 2 * size
    tiles_j = quarter // LANES
    tiles_n = total // LANES
    half_n = total // 2
    half = LANES // 2
    whole = 2 * rows + size
    highest = lax.Precision.HIGHEST
    f32, bf16 = jnp.float32, jnp.bfloat16
    w = lax.axis_index("wave")
    x = lax.axis_index("lev")
    right, left, far = lax.rem(x + 1, nx), lax.rem(x + nx - 1, nx), lax.rem(x + 2, nx)
    chunks = (CHUNKS_IN, CHUNKS_OUT)

    def remote(src, dst, send, recv, to_w, to_x):
        return pltpu.make_async_remote_copy(
            src_ref=src,
            dst_ref=dst,
            send_sem=send,
            recv_sem=recv,
            device_id=(to_w, to_x),
            device_id_type=MESH,
        )

    def drain(ref, sem):
        pltpu.make_async_copy(ref, ref, sem).wait()

    barrier = pltpu.get_barrier_semaphore()

    @pl.loop(1, nw)
    def _(k):
        pl.semaphore_signal(
            barrier, inc=1, device_id=(lax.rem(w + k, nw), x), device_id_type=MESH
        )

    for k in range(1, nx):
        pl.semaphore_signal(
            barrier, inc=1, device_id=(w, lax.rem(x + k, nx)), device_id_type=MESH
        )

    def field_copies(r):
        parts = [pl.ds((2 * c + r) * lev * band, lev * band) for c in range(2)]
        return [
            pltpu.make_async_copy(fourier.at[at, :], field.at[at, :], field_sem.at[r, c])
            for c, at in enumerate(parts)
        ]

    for r in range(2):
        for copy in field_copies(r):
            copy.start()

    small_copies = [
        pltpu.make_async_copy(source, target, small_sem.at[i])
        for i, (source, target) in enumerate(
            (
                (weights_far, weights),
                (points_far, points),
                (zonal_far, zonal),
                (balance_far, balance),
                (modes_far, modes),
                (project_far, project),
                (eigen_far, eigen),
                (reply_far, reply),
                (pick_div_far, pick_div),
                (pick_temp_far, pick_temp),
                (place_div_far, place_div),
                (place_temp_far, place_temp),
            )
        )
    ]
    for copy in small_copies:
        copy.start()
    leg_copies = [
        pltpu.make_async_copy(legendre.at[s], leg_full.at[s], leg_sem.at[s])
        for s in range(2)
    ]
    for copy in leg_copies:
        copy.start()

    def own_zonal(s):
        places = lax.broadcasted_iota(jnp.int32, zonal.shape, 1)
        return jnp.sum(
            jnp.where(places == 2 * w + s, zonal[...], 0), axis=1, keepdims=True
        )

    def masks():
        for s in range(2):
            for t in range(tiles_j):
                at = pl.ds(x * tiles_j + t, 1)
                here = 2 * own_zonal(s) < points[at, :]
                row = slice(s * tiles_j + t, s * tiles_j + t + 1)
                mask_weight[row, :] = jnp.where(here, weights[at, :], 0.0)
                mask_present[row, :] = jnp.where(here, 1.0, 0.0)

    def first_row(r, k):
        c, third = k // thirds, k % thirds
        return pl.multiple_of(((2 * c + r) * lev + per * third) * band, 8)

    def spread(r, low, high):
        if low == 0:
            for copy in field_copies(r):
                copy.wait()

        @pl.loop(low, high)
        def _(k):
            block = field[pl.ds(first_row(r, k), per * band), :]
            block = jnp.concatenate(
                [block, jnp.zeros((LANES - per * band, LANES), f32)], axis=0
            )
            out_rows[r, pl.ds(k, 2 * nw, stride=pairs), :] = block.T

    def from_wave(index, chunk):
        first, n = chunk
        return pl.ds(pl.multiple_of(nw * first + index * n, 8), n)

    def all_waves(chunk, count=nw):
        first, n = chunk
        return pl.ds(nw * first, count * n)

    def wave_exchange(kind, r, c, source, target):
        send, recv = wave_send.at[kind, r, c], wave_recv.at[kind, r, c]

        @pl.loop(1, nw)
        def _(k):
            to = lax.rem(w + k, nw)
            remote(source(to), target, send, recv, to, x).start()

        pltpu.make_async_copy(source(w), target, recv).start()

    def wave_in(r, c):
        chunk = chunks[0][r][c]
        first, n = chunk
        wave_exchange(
            0,
            r,
            c,
            lambda to: out_rows.at[r, pl.ds(pl.multiple_of(to * groups + first, 8), n), :],
            in_rows.at[r, from_wave(w, chunk), :],
        )

    def wave_in_wait(r, c):
        drain(in_rows.at[r, all_waves(chunks[0][r][c]), :], wave_recv.at[0, r, c])

    def wave_out(r, c):
        chunk = chunks[1][r][c]
        wave_exchange(
            1,
            r,
            c,
            lambda to: returned.at[r, from_wave(to, chunk), :],
            final.at[r, from_wave(w, chunk), :],
        )

    def wave_out_wait(r, c):
        drain(final.at[r, all_waves(chunks[1][r][c]), :], wave_recv.at[1, r, c])

    def span(q, chunk):
        first, n = chunk
        return pl.ds(pl.multiple_of(nw * first + q * (near * n), 8), near * n)

    def lev_start(kind, r, c):
        source, target = ((in_rows, blocks), (packed, returned))[kind]
        chunk = chunks[kind][r][c]
        send, recv = lev_send.at[kind, r, c], lev_recv.at[kind, r, c]
        for to in (far, right, left):
            remote(
                source.at[r, span(to, chunk), :],
                target.at[r, span(x, chunk), :],
                send,
                recv,
                w,
                to,
            ).start()
        pltpu.make_async_copy(
            source.at[r, span(x, chunk), :], target.at[r, span(x, chunk), :], recv
        ).start()

    def lev_wait(kind, r, c):
        target = (blocks, returned)[kind]
        drain(target.at[r, all_waves(chunks[kind][r][c]), :], lev_recv.at[kind, r, c])

    def unpack(r, c):
        chunk = chunks[0][r][c]
        first, n = chunk
        lane = lax.broadcasted_iota(jnp.int32, (n, LANES), 1)

        @pl.loop(0, nx)
        def _(lg):
            bands = [
                blocks[r, from_wave(lg * near + b, chunk), :]
                for b in range(near)
            ]
            for i in range(per):
                at = pl.ds(first * cells + lg * per + i, n, stride=cells)
                for t in range(tiles_j):
                    value = None
                    for b in range(near):
                        low = b * band - t * LANES
                        if low + band <= 0 or low >= LANES:
                            continue
                        turn = (low - i * band) % LANES
                        moved = pltpu.roll(bands[b], turn, 1) if turn else bands[b]
                        value = moved if value is None else jnp.where(lane >= low, moved, value)
                    planes_in[t, at, :] = value

    def places(parts, u):
        before = [0, 0]
        for v, (first, count) in enumerate(parts):
            start, m = first * cells, count * cells
            offset, length = start * 5 // 2, m * 5 // 2
            cut = (length // 2 + 7) // 8 * 8
            if v == u:
                return (
                    (start, m, offset),
                    pl.ds(offset, cut),
                    pl.ds(offset + cut, length - cut),
                    pl.ds(before[0], cut),
                    pl.ds(before[1], length - cut),
                )
            before = [before[0] + cut, before[1] + length - cut]

    def analysis(p, u, h):
        s = p % 2
        start, m, offset = places(PARTS_SUM[p], u)[0]
        n_at = pl.ds(pl.multiple_of(h * half_n, 16), half_n)
        a_hi, a_lo = grid_hi[start : start + m, :], grid_lo[start : start + m, :]
        b_hi, b_lo = leg_hi[s, n_at, :], leg_lo[s, n_at, :]
        dot = functools.partial(
            lax.dot_general,
            dimension_numbers=(((1,), (1,)), ((), ())),
            preferred_element_type=f32,
        )
        value = dot(a_hi, b_hi) + (dot(a_hi, b_lo) + dot(a_lo, b_hi))
        low = lax.broadcasted_iota(jnp.int32, (m // 2, LANES), 1) < half
        even, odd = 2 * h, 2 * h + 1
        one, two, three = (pl.ds(offset, m), pl.ds(offset + m, m), pl.ds(offset + 2 * m, m // 2))
        partial[p, even, one, :] = value[:, 0:LANES]
        partial[p, even, two, :] = value[:, LANES : 2 * LANES]
        middle = value[:, 2 * LANES : 3 * LANES]
        first, second = middle[: m // 2], middle[m // 2 :]
        partial[p, even, three, :] = jnp.where(low, first, pltpu.roll(second, half, 1))
        partial[p, odd, three, :] = jnp.where(low, pltpu.roll(first, half, 1), second)
        partial[p, odd, one, :] = value[:, 3 * LANES : 4 * LANES]
        partial[p, odd, two, :] = value[:, 4 * LANES : 5 * LANES]

    def reduce_start(p, u):
        s = p % 2
        (start, m, _), top, bottom, at_a, at_b = places(PARTS_SUM[p], u)
        for t in range(tiles_j):
            value = planes_in[t, s * rows + start : s * rows + start + m, :]
            value = value * mask_weight[s * tiles_j + t : s * tiles_j + t + 1, :]
            high = value.astype(bf16)
            lanes = slice(t * LANES, (t + 1) * LANES)
            grid_hi[start : start + m, lanes] = high
            grid_lo[start : start + m, lanes] = (value - high.astype(f32)).astype(bf16)
        send, recv = sum_send.at[p], sum_recv.at[p, u]
        analysis(p, u, far // 2)
        remote(partial.at[p, far, top], sum_a.at[p, at_a], send, recv.at[0], w, right).start()
        remote(partial.at[p, far, bottom], sum_b.at[p, at_b], send, recv.at[1], w, left).start()
        analysis(p, u, x // 2)
        remote(
            partial.at[p, right, bottom], sum_left.at[p, bottom], send, recv.at[2], w, right
        ).start()
        remote(partial.at[p, left, top], sum_right.at[p, top], send, recv.at[3], w, left).start()

    def reduce_forward(p, u):
        _, top, bottom, at_a, at_b = places(PARTS_SUM[p], u)
        send, recv = sum_send.at[p], sum_recv.at[p, u]
        drain(sum_a.at[p, at_a], recv.at[0])
        partial[p, right, top, :] += sum_a[p, at_a, :]
        remote(partial.at[p, right, top], sum_left.at[p, top], send, recv.at[4], w, right).start()
        drain(sum_b.at[p, at_b], recv.at[1])
        partial[p, left, bottom, :] += sum_b[p, at_b, :]
        remote(
            partial.at[p, left, bottom], sum_right.at[p, bottom], send, recv.at[5], w, left
        ).start()

    def solve(p):
        s = p % 2
        pieces = []
        for u in range(len(PARTS_SUM[p])):
            (_, m, offset), top, bottom, _, _ = places(PARTS_SUM[p], u)
            recv = sum_recv.at[p, u]
            drain(sum_left.at[p, bottom], recv.at[2])
            drain(sum_right.at[p, top], recv.at[3])
            drain(sum_left.at[p, top], recv.at[4])
            drain(sum_right.at[p, bottom], recv.at[5])
            at = pl.ds(offset, m * 5 // 2)
            value = partial[p, x, at, :] + (sum_left[p, at, :] + sum_right[p, at, :])
            last = value[2 * m :]
            pieces.append(
                jnp.concatenate(
                    [
                        value[:m],
                        value[m : 2 * m],
                        jnp.concatenate([last, pltpu.roll(last, half, 1)], axis=0),
                    ],
                    axis=1,
                )
            )
        value = pieces[0] if len(pieces) == 1 else jnp.concatenate(pieces, axis=0)
        lanes = lax.broadcasted_iota(jnp.int32, (1, LANES), 1)
        begin, odd = (x // 2) * half_n, x % 2
        first = begin + odd * (half_n - 2 * LANES) + lanes
        middle = begin + 2 * LANES + odd * half + lanes % half
        n = jnp.concatenate([first, first + LANES, middle], axis=1)
        value = jnp.where(n >= own_zonal(s), value, 0.0)
        factor = (n * (n + 1)).astype(f32) * (4.0 / (total * (total + 1)))
        both = jnp.dot(modal_in[...], value, precision=highest, preferred_element_type=f32)
        diagonal = lax.broadcasted_iota(jnp.int32, (size, size), 0) == lax.broadcasted_iota(
            jnp.int32, (size, size), 1
        )
        depth = jnp.sum(jnp.where(diagonal, eigen[...], 0.0), axis=1, keepdims=True)
        modal = (both[:size] + factor * both[size:]) / (1.0 + depth * factor)
        answer = jnp.dot(modal_out[...], modal, precision=highest, preferred_element_type=f32)
        thermal = lax.broadcasted_iota(jnp.int32, (rows, 1), 0) >= size
        answer = answer + jnp.where(thermal, value, 0.0)
        for u in range(len(PARTS_GATHER[p])):
            start, m, offset = places(PARTS_GATHER[p], u)[0]
            low = lax.broadcasted_iota(jnp.int32, (m // 2, LANES), 1) < half
            part = answer[start : start + m]
            solved[p, x, pl.ds(offset, m), :] = part[:, :LANES]
            solved[p, x, pl.ds(offset + m, m), :] = part[:, LANES : 2 * LANES]
            last = part[:, 2 * LANES :]
            solved[p, x, pl.ds(offset + 2 * m, m // 2), :] = jnp.where(
                low, last[: m // 2], pltpu.roll(last[m // 2 :], half, 1)
            )

    def gather_start(p):
        send = gather_send.at[p]
        for u in range(len(PARTS_GATHER[p])):
            halves = places(PARTS_GATHER[p], u)[1:3]
            for step in range(2):
                for to, first in ((right, 0), (left, 1)):
                    part = (first, 1 - first)[step]
                    block = solved.at[p, x, halves[part]]
                    remote(
                        block, block, send, gather_recv.at[p, u, 2 * first + part], w, to
                    ).start()

    def gather_forward(p, u):
        _, top, bottom, _, _ = places(PARTS_GATHER[p], u)
        send, recv = gather_send.at[p], gather_recv.at[p, u]
        for block, got, index, to in (
            (solved.at[p, left, top], 0, 4, right),
            (solved.at[p, right, bottom], 3, 5, left),
        ):
            drain(block, recv.at[got])
            remote(block, block, send, recv.at[index], w, to).start()

    def gather_wait(p, u):
        _, top, bottom, _, _ = places(PARTS_GATHER[p], u)
        recv = gather_recv.at[p, u]
        drain(solved.at[p, left, bottom], recv.at[1])
        drain(solved.at[p, right, top], recv.at[2])
        drain(solved.at[p, far, top], recv.at[4])
        drain(solved.at[p, far, bottom], recv.at[5])

    def synthesis(p, u):
        s = p % 2
        start, m, offset = places(PARTS_GATHER[p], u)[0]
        low = lax.broadcasted_iota(jnp.int32, (m // 2, LANES), 1) < half
        one, two, three = (pl.ds(offset, m), pl.ds(offset + m, m), pl.ds(offset + 2 * m, m // 2))
        at, upper, lower = (pl.ds(start, m), pl.ds(start, m // 2), pl.ds(start + m // 2, m // 2))
        for h in range(2):
            even, odd, t = 2 * h, 2 * h + 1, h * (tiles_n // 2)
            mixed[t, at, :] = solved[p, even, one, :]
            mixed[t + 1, at, :] = solved[p, even, two, :]
            before, after = solved[p, even, three, :], solved[p, odd, three, :]
            mixed[t + 2, upper, :] = jnp.where(low, before, pltpu.roll(after, half, 1))
            mixed[t + 2, lower, :] = jnp.where(low, pltpu.roll(before, half, 1), after)
            mixed[t + 3, at, :] = solved[p, odd, one, :]
            mixed[t + 4, at, :] = solved[p, odd, two, :]
        for t in range(tiles_n):
            value = mixed[t, at, :]
            high = value.astype(bf16)
            lanes = slice(t * LANES, (t + 1) * LANES)
            spec_hi[start : start + m, lanes] = high
            spec_lo[start : start + m, lanes] = (value - high.astype(f32)).astype(bf16)
        a_hi, a_lo = spec_hi[start : start + m, :], spec_lo[start : start + m, :]
        begin = 0
        while begin < quarter:
            width = min(256, quarter - begin)
            b_hi = leg_hi[s, :, begin : begin + width]
            b_lo = leg_lo[s, :, begin : begin + width]
            dot = functools.partial(jnp.dot, preferred_element_type=f32)
            value = dot(a_hi, b_hi) + (dot(a_hi, b_lo) + dot(a_lo, b_hi))
            for t in range(width // LANES):
                tile = begin // LANES + t
                row = s * tiles_j + tile
                here = mask_present[row : row + 1, :] > 0.5
                planes_out[tile, pl.ds(s * rows + start, m), :] = jnp.where(
                    here, value[:, t * LANES : (t + 1) * LANES], 0.0
                )
            begin += width

    def write_spectral(p, u):
        r, s = p // 2, p % 2
        first, count = PARTS_GATHER[p][u]
        for t in range(tiles_n):
            for i in range(per):
                for k in range(first, first + count):
                    c, third = k // thirds, k % thirds
                    spec_rows[
                        s,
                        per * third + i,
                        2 * c + r : 2 * c + r + 1,
                        t * LANES : (t + 1) * LANES,
                    ] = mixed[t, pl.ds(k * cells + x * per + i, 1), :]

    def pack(r, c):
        chunk = chunks[1][r][c]
        first, n = chunk
        lane = lax.broadcasted_iota(jnp.int32, (n, LANES), 1)

        @pl.loop(0, nx)
        def _(lg):
            tiles = [
                [
                    planes_out[t, pl.ds(first * cells + lg * per + i, n, stride=cells), :]
                    for t in range(tiles_j)
                ]
                for i in range(per)
            ]
            for b in range(near):
                value = None
                for i in range(per):
                    t, low = (b * band) // LANES, (b * band) % LANES
                    turn = (i * band - low) % LANES
                    moved = tiles[i][t]
                    moved = pltpu.roll(moved, turn, 1) if turn else moved
                    if low + band > LANES:
                        other = tiles[i][t + 1]
                        other = pltpu.roll(other, turn, 1) if turn else other
                        moved = jnp.where(lane >= i * band + LANES - low, other, moved)
                    value = moved if value is None else jnp.where(lane >= i * band, moved, value)
                packed[r, from_wave(lg * near + b, chunk), :] = value

    def write_back(r, c):
        at = pl.ds((2 * c + r) * lev * band, lev * band)
        return pltpu.make_async_copy(result.at[at, :], fourier_new.at[at, :], out_sem.at[r, c])

    def collect(r):
        for k in range(pairs):
            for s in range(2):
                at = s * pairs + k
                first, n = next(chunk for chunk in chunks[1][r] if at < sum(chunk))
                square[k % 2, pl.ds(s, nw, stride=2), :] = final[
                    r, pl.ds(nw * first + at - first, nw, stride=n), :
                ]
            result[pl.ds(first_row(r, k), per * band), :] = square[k % 2].T[: per * band]
            if k % thirds == thirds - 1:
                write_back(r, k // thirds).start()

    def split(s):
        leg_copies[s].wait()
        chunk = 64

        @pl.loop(0, total // chunk)
        def _(k):
            at = pl.ds(pl.multiple_of(k * chunk, chunk), chunk)
            value = leg_full[s, at, :]
            high = value.astype(bf16)
            leg_hi[s, at, :] = high
            leg_lo[s, at, :] = (value - high.astype(f32)).astype(bf16)

    def matrices():
        for copy in small_copies:
            copy.wait()
        masks()
        exact = functools.partial(jnp.dot, precision=highest, preferred_element_type=f32)
        modal_in[:size, :] = exact(project[...], pick_div[...])
        modal_in[size:, :] = exact(exact(project[...], balance[...]), pick_temp[...])
        modal_out[...] = exact(place_div[...], modes[...]) - exact(
            place_temp[...], exact(reply[...], modes[...])
        )

    spread(0, 0, chunks[0][0][0][1])
    pl.semaphore_wait(barrier, nw - 1 + nx - 1)
    wave_in(0, 0)
    spread(0, chunks[0][0][0][1], pairs)
    split(0)
    wave_in(0, 1)
    wave_in(0, 2)
    matrices()
    wave_in_wait(0, 0)
    spread(1, 0, pairs)
    lev_start(0, 0, 0)
    wave_in_wait(0, 1)
    lev_start(0, 0, 1)
    wave_in(1, 1)
    wave_in(1, 0)
    lev_wait(0, 0, 0)
    unpack(0, 0)
    reduce_start(0, 0)
    lev_wait(0, 0, 1)
    unpack(0, 1)
    wave_in_wait(0, 2)
    lev_start(0, 0, 2)
    wave_in(1, 2)
    reduce_forward(0, 0)
    reduce_start(0, 1)
    split(1)
    wave_in_wait(1, 1)
    lev_start(0, 1, 1)
    lev_wait(0, 0, 2)
    unpack(0, 2)
    reduce_forward(0, 1)
    reduce_start(1, 0)
    solve(0)
    wave_in_wait(1, 0)
    gather_start(0)
    reduce_forward(1, 0)
    lev_start(0, 1, 0)
    lev_wait(0, 1, 1)
    gather_forward(0, 0)
    wave_in_wait(1, 2)
    unpack(1, 1)
    solve(1)
    lev_start(0, 1, 2)
    gather_start(1)
    gather_wait(0, 0)
    lev_wait(0, 1, 0)
    synthesis(0, 0)
    unpack(1, 0)
    pack(0, 0)
    reduce_start(2, 0)
    gather_forward(1, 0)
    lev_start(1, 0, 0)
    write_spectral(0, 0)
    lev_wait(0, 1, 2)
    unpack(1, 2)
    reduce_start(3, 0)
    gather_wait(1, 0)
    reduce_forward(2, 0)
    lev_wait(1, 0, 0)
    synthesis(1, 0)
    pack(0, 1)
    lev_start(1, 0, 1)
    reduce_forward(3, 0)
    write_spectral(1, 0)
    wave_out(0, 0)
    solve(2)
    pack(0, 2)
    gather_start(2)
    lev_wait(1, 0, 1)
    lev_start(1, 0, 2)
    gather_forward(2, 0)
    solve(3)
    wave_out(0, 1)
    gather_start(3)
    lev_wait(1, 0, 2)
    wave_out(0, 2)
    gather_wait(2, 0)
    synthesis(2, 0)
    gather_forward(3, 0)
    pack(1, 0)
    lev_start(1, 1, 0)
    write_spectral(2, 0)
    gather_wait(3, 0)
    synthesis(3, 0)
    wave_out_wait(0, 1)
    gather_forward(3, 1)
    pack(1, 1)
    lev_start(1, 1, 1)
    lev_wait(1, 1, 0)
    wave_out(1, 0)
    gather_wait(3, 1)
    wave_out_wait(0, 0)
    synthesis(3, 1)
    pack(1, 2)
    wave_out_wait(0, 2)
    lev_start(1, 1, 2)
    write_spectral(3, 0)
    write_spectral(3, 1)
    lev_wait(1, 1, 1)
    wave_out(1, 1)
    collect(0)
    lev_wait(1, 1, 2)
    spec_copy = pltpu.make_async_copy(spec_rows, spectral, out_sem.at[0, 2])
    spec_copy.start()
    wave_out(1, 2)

    for kind in range(2):
        for r in range(2):
            for c, chunk in enumerate(chunks[kind][r]):
                drain(in_rows.at[r, all_waves(chunk, nw - 1), :], wave_send.at[kind, r, c])
                sent = nw - near
                drain(in_rows.at[r, all_waves(chunk, sent), :], lev_send.at[kind, r, c])
    for p in range(4):
        drain(solved.at[p, pl.ds(0, 3)], sum_send.at[p])
        drain(solved.at[p, pl.ds(0, 3)], gather_send.at[p])
    for c in range(len(chunks[1][1])):
        wave_out_wait(1, c)
    collect(1)
    spec_copy.wait()
    for r in range(2):
        for c in range(2):
            write_back(r, c).wait()


def on_device(
    nw,
    nx,
    fourier,
    legendre,
    weights,
    points,
    zonal,
    pressure_balance_matrix,
    modes,
    project,
    eigen,
    thermal_reply_matrix,
):
    waves, parts, lev, band = fourier.shape
    slots, total, quarter = legendre.shape
    size = nx * lev
    per = LANES // band
    groups = parts * lev // per
    rows = 2 * size
    whole = 2 * rows + size
    cut = (whole // 2 + 7) // 8 * 8
    tiles_n = total // LANES
    dims = (nw, nx, band, lev, total, quarter)

    pick = np.zeros((2, size, rows), np.float32)
    row = 0
    for c in range(2):
        for third in range(lev // per):
            for group in range(nx):
                for i in range(per):
                    pick[c, group * lev + per * third + i, row] = 1.0
                    row += 1

    view = fourier.transpose(1, 2, 3, 0).reshape(parts * lev * band, waves)
    f32, bf16 = jnp.float32, jnp.bfloat16
    anywhere = pl.BlockSpec(memory_space=pl.ANY)
    dma = pltpu.SemaphoreType.DMA
    lines = pltpu.VMEM((2, nw * groups, LANES), f32)
    spectral, fourier_new = pl.pallas_call(
        functools.partial(kernel, dims),
        out_shape=(
            jax.ShapeDtypeStruct((slots, lev, parts, total), f32),
            jax.ShapeDtypeStruct(view.shape, f32),
        ),
        in_specs=[anywhere] * 14,
        out_specs=(anywhere, anywhere),
        scratch_shapes=[
            pltpu.VMEM((weights.shape[0] // LANES, LANES), f32),
            pltpu.VMEM((weights.shape[0] // LANES, LANES), jnp.int32),
            pltpu.VMEM((1, waves), jnp.int32),
            pltpu.VMEM((size, size), f32),
            pltpu.VMEM((size, size), f32),
            pltpu.VMEM((size, size), f32),
            pltpu.VMEM((1, size), f32),
            pltpu.VMEM((size, size), f32),
            pltpu.VMEM((size, rows), f32),
            pltpu.VMEM((size, rows), f32),
            pltpu.VMEM((rows, size), f32),
            pltpu.VMEM((rows, size), f32),
            pltpu.VMEM(view.shape, f32),
            pltpu.VMEM((slots, total, quarter), f32),
            pltpu.VMEM((slots, total, quarter), bf16),
            pltpu.VMEM((slots, total, quarter), bf16),
            pltpu.VMEM((2 * (quarter // LANES), LANES), f32),
            pltpu.VMEM((2 * (quarter // LANES), LANES), f32),
            pltpu.VMEM((2, LANES, LANES), f32),
            lines,
            lines,
            lines,
            pltpu.VMEM((quarter // LANES, 2 * rows, LANES), f32),
            pltpu.VMEM((quarter // LANES, 2 * rows, LANES), f32),
            pltpu.VMEM((rows, quarter), bf16),
            pltpu.VMEM((rows, quarter), bf16),
            pltpu.VMEM((4, nx, whole, LANES), f32),
            pltpu.VMEM((4, cut, LANES), f32),
            pltpu.VMEM((4, cut, LANES), f32),
            pltpu.VMEM((4, whole, LANES), f32),
            pltpu.VMEM((4, whole, LANES), f32),
            pltpu.VMEM((rows, rows), f32),
            pltpu.VMEM((rows, size), f32),
            pltpu.VMEM((4, nx, whole, LANES), f32),
            pltpu.VMEM((tiles_n, rows, LANES), f32),
            pltpu.VMEM((rows, total), bf16),
            pltpu.VMEM((rows, total), bf16),
            pltpu.VMEM((slots, lev, parts, total), f32),
            lines,
            lines,
            lines,
            pltpu.VMEM(view.shape, f32),
            dma((12,)),
            dma((2, 2)),
            dma((2,)),
            dma((2, 2, 3)),
            dma((2, 2, 3)),
            dma((2, 2, 3)),
            dma((2, 2, 3)),
            dma((4,)),
            dma((4, 2, 6)),
            dma((4,)),
            dma((4, 2, 6)),
            dma((2, 3)),
        ],
        compiler_params=pltpu.CompilerParams(
            collective_id=0, has_side_effects=True, vmem_limit_bytes=58 * 1024 * 1024
        ),
    )(
        view,
        legendre,
        weights.reshape(-1, LANES),
        points.reshape(-1, LANES),
        zonal.reshape(1, waves),
        pressure_balance_matrix,
        modes,
        project,
        eigen.reshape(1, size),
        thermal_reply_matrix,
        jnp.asarray(pick[0]),
        jnp.asarray(pick[1]),
        jnp.asarray(pick[0].T),
        jnp.asarray(pick[1].T),
    )
    spectral = spectral.transpose(0, 2, 1, 3)
    fourier_new = fourier_new.reshape(parts, lev, band, waves).transpose(3, 0, 1, 2)
    return (spectral, fourier_new)


def solution(mesh):
    return jax.shard_map(
        functools.partial(on_device, mesh.shape["wave"], mesh.shape["lev"]),
        mesh=mesh,
        in_specs=(
            P(None, None, "lev", "wave"),
            P("wave", None, "lev"),
            P(),
            P(),
            P(),
            P(),
            P(),
            P(),
            P(),
            P(),
        ),
        out_specs=(P("wave", None, "lev", None), P(None, None, "lev", "wave")),
        check_vma=False,
    )
```

time: 135 us -> 131 us (0.970)
  Pallas kernels: 131 us -> 127 us
    pallas_call x1, Pallas kernels: 131 us -> 127 us  [on_device(): pl.pallas_call(functools.partial(kernel, dims), out_shape=(jax.ShapeDtype...]
where the time goes in v3:
time: 131 us; the launch traced here: 130 us
  Pallas kernels  127 us (97%)
  local copies, waits for them, and re-layouts  3.25 us (2%)
    pallas_call x1, Pallas kernels, on_device(): pl.pallas_call(functools.partial(kernel, dims), out_shape=(jax.ShapeDtype...  127 us
    unnamed x4, local copies, waits for them, and re-layouts  3.25 us

profile of v3, /device:TPU:1, one launch (start us, length us, event | category | flops | bytes accessed | tf_op | source)
XLA Modules:
  0.0 130.4 jit_solution(13944688489405319841)
XLA Ops:
  0.6 126.5 %shard_map.149 = (f32[2,18,4,1280]{3,2,1,0:T(4,128)}, f32[2880,128]{1,0:T(8,128)}) custom-call(f32[2880,128]{1,0:T(8,128)} %bitcast.11, f32[2,1280,640]{2,1,0:T(8,128)} %legendre.1, f32[20,128]{1,0:T(8,128)} %bitcast.14, s32[20,128]{1,0:T(8,128)} %bitcast.15, s32[1,128]{1,0:T(1,128)} %bitcast.16, f32[72,72]{1,0:T(8,128)} %balance_far.1, f32[72,72]{1,0:T(8,128)} %modes_far.1, ...), custom_call_target="tpu_custom_call" | custom-call | tf_op jit(solution)/shard_map/pallas_call | solution.py:740
  127.2 0.0 copy-start
  127.2 2.1 %copy.18 = f32[2,4,18,1280]{3,1,2,0:T(4,128)} copy(f32[2,4,18,1280]{3,1,2,0:T(4,128)} %bitcast.13) | data formatting | bytes 1474560
  129.3 0.0 copy-done
  129.3 1.1 copy.19
Async XLA Ops:
  127.2 2.2 %copy-start = (f32[2880,128]{1,0:T(8,128)S(1)}, f32[2880,128]{1,0:T(8,128)}, u32[]{:S(2)}) copy-start(f32[2880,128]{1,0:T(8,128)} %get-tuple-element.5) | copy-start | bytes 4423684

commit v4 on v3

--- a/solution.py
+++ b/solution.py
@@ -658,27 +658,27 @@
     write_spectral(2, 0)
     gather_wait(3, 0)
     synthesis(3, 0)
-    wave_out_wait(0, 1)
     gather_forward(3, 1)
     pack(1, 1)
     lev_start(1, 1, 1)
     lev_wait(1, 1, 0)
     wave_out(1, 0)
     gather_wait(3, 1)
-    wave_out_wait(0, 0)
     synthesis(3, 1)
     pack(1, 2)
-    wave_out_wait(0, 2)
     lev_start(1, 1, 2)
+    lev_wait(1, 1, 1)
+    wave_out(1, 1)
+    lev_wait(1, 1, 2)
+    wave_out(1, 2)
     write_spectral(3, 0)
     write_spectral(3, 1)
-    lev_wait(1, 1, 1)
-    wave_out(1, 1)
-    collect(0)
-    lev_wait(1, 1, 2)
     spec_copy = pltpu.make_async_copy(spec_rows, spectral, out_sem.at[0, 2])
     spec_copy.start()
-    wave_out(1, 2)
+    wave_out_wait(0, 0)
+    wave_out_wait(0, 1)
+    wave_out_wait(0, 2)
+    collect(0)
 
     for kind in range(2):
         for r in range(2):
@@ -696,6 +696,29 @@
     for r in range(2):
         for c in range(2):
             write_back(r, c).wait()
+
+
+def hand_on(parts, spectral_raw, fourier_raw, spectral, fourier_new, low, high, sems):
+    rows = fourier_raw.shape[0] // parts
+    blocks = [pl.ds(i * rows, rows) for i in range(parts)]
+    routes = [
+        (fourier_raw.at[at, :], low.at[at, :], fourier_new.at[at, :]) for at in blocks
+    ] + [(spectral_raw.at[s], high.at[s], spectral.at[s]) for s in range(spectral.shape[0])]
+    arrivals = [
+        pltpu.make_async_copy(source, held, sems.at[0, i])
+        for i, (source, held, _) in enumerate(routes)
+    ]
+    departures = [
+        pltpu.make_async_copy(held, target, sems.at[1, i])
+        for i, (_, held, target) in enumerate(routes)
+    ]
+    for copy in arrivals:
+        copy.start()
+    for first, second in zip(arrivals, departures):
+        first.wait()
+        second.start()
+    for copy in departures:
+        copy.wait()
 
 
 def on_device(
@@ -820,6 +843,20 @@
         jnp.asarray(pick[0].T),
         jnp.asarray(pick[1].T),
     )
+    spectral, fourier_new = pl.pallas_call(
+        functools.partial(hand_on, 4),
+        out_shape=(
+            jax.ShapeDtypeStruct(spectral.shape, f32),
+            jax.ShapeDtypeStruct(fourier_new.shape, f32),
+        ),
+        in_specs=[anywhere] * 2,
+        out_specs=(anywhere, anywhere),
+        scratch_shapes=[
+            pltpu.VMEM(fourier_new.shape, f32),
+            pltpu.VMEM(spectral.shape, f32),
+            dma((2, 4 + slots)),
+        ],
+    )(spectral, fourier_new)
     spectral = spectral.transpose(0, 2, 1, 3)
     fourier_new = fourier_new.reshape(parts, lev, band, waves).transpose(3, 0, 1, 2)
     return (spectral, fourier_new)

time: 131 us -> 129 us (0.985)
  local copies, waits for them, and re-layouts: 3.25 us -> 0 us
    unnamed x4 -> x0, local copies, waits for them, and re-layouts: 3.25 us -> none
    pallas_call x0 -> x1, Pallas kernels: none -> 2.44 us  [on_device(): pl.pallas_call(functools.partial(hand_on, 4), out_shape=(jax.ShapeDtypeSt...]
where the time goes in v4:
time: 129 us
  Pallas kernels  128 us (99%)
    pallas_call x1, Pallas kernels, on_device(): pl.pallas_call(functools.partial(kernel, dims), out_shape=(jax.ShapeDtype...  126 us

profile of v4, /device:TPU:1, one launch (start us, length us, event | category | flops | bytes accessed | tf_op | source)
XLA Modules:
  0.0 129.2 jit_solution(12561461588085384418)
XLA Ops:
  0.6 126.0 %shard_map.149 = (f32[2,18,4,1280]{3,2,1,0:T(4,128)}, f32[2880,128]{1,0:T(8,128)}) custom-call(f32[2880,128]{1,0:T(8,128)} %bitcast.11, f32[2,1280,640]{2,1,0:T(8,128)} %legendre.1, f32[20,128]{1,0:T(8,128)} %bitcast.12, s32[20,128]{1,0:T(8,128)} %bitcast.13, s32[1,128]{1,0:T(1,128)} %bitcast.14, f32[72,72]{1,0:T(8,128)} %balance_far.1, f32[72,72]{1,0:T(8,128)} %modes_far.1, ...), custom_call_target="tpu_custom_call" | custom-call | tf_op jit(solution)/shard_map/pallas_call | solution.py:763
  126.6 2.4 %shard_map.150 = (f32[2,18,4,1280]{3,2,1,0:T(4,128)}, f32[2880,128]{1,0:T(8,128)}) custom-call(f32[2,18,4,1280]{3,2,1,0:T(4,128)} %get-tuple-element.6.spectral_raw, f32[2880,128]{1,0:T(8,128)} %get-tuple-element.7.fourier_raw), custom_call_target="tpu_custom_call" | custom-call | tf_op jit(solution)/shard_map/pallas_call | solution.py:846
